TPU v7x, 512 devices: a whole 4x4x16 slice. The times are simulated.
512 devices in a mesh: ex: 64 (over x_hi, z, core), feat: 8 (over y, x_lo).
Axes of the slice: x: 4 (x_hi: 2, x_lo: 2; x = x_hi * 2 + x_lo), y: 4, z: 16, core: 2. Of those that a mesh axis runs over, the one named last changes fastest.
Arguments:
- features: bfloat16 [6144, 8192], P('ex', 'feat'), may hold values from -100 to 100
Outputs:
- kernel: float32 [6144, 6144], P('ex', 'feat')
All inputs are finite; a program needn't handle non-finite values.
Results may differ from a plain program's by a relative error of at most 0.0003.
Values may be sent and summed in bfloat16 or wider, within the bound.
No kernel may reach another device: no remote copies, remote signals or barrier semaphores. Data moves between devices by JAX's collectives and lax.ppermute only.
A program may use at most 64 MiB of HBM per device.

v0:
```python
import jax
import jax.numpy as jnp
from jax import lax
from jax.sharding import PartitionSpec as P


def inner_tile(left, right):
    return lax.dot_general(
        left, right, (((1,), (1,)), ((), ())), preferred_element_type=jnp.float32
    )


def shards(features):
    local_squares = jnp.sum(jnp.square(features.astype(jnp.float32)), axis=1)
    row_norms = lax.psum(local_squares, "feat")
    every_norm = lax.all_gather(row_norms, "ex", axis=0, tiled=True)
    partial_gram = inner_tile(features, lax.all_gather(features, "ex", axis=0, tiled=True))
    gram = lax.psum_scatter(partial_gram, "feat", scatter_dimension=1, tiled=True)
    col_width = gram.shape[1]
    col_norms = lax.dynamic_slice_in_dim(
        every_norm, lax.axis_index("feat") * col_width, col_width, 0
    )
    row_scale = lax.rsqrt(row_norms + 1e-06)
    col_scale = lax.rsqrt(col_norms + 1e-06)
    return gram * row_scale[:, None] * col_scale[None, :]


def solution(mesh):
    placed = (P("ex", "feat"),)
    return jax.shard_map(
        shards, mesh=mesh, in_specs=placed, out_specs=P("ex", "feat"), check_vma=False
    )
```

profile of v0, /device:TPU:1, one launch (start us, length us, event | category | flops | bytes accessed | tf_op | source)
XLA Modules:
  0.0 487.4 jit_solution(17490447858818020468)
XLA Ops:
  6.5 0.0 copy-start
  6.5 0.0 all-gather.2.cloned.1.call-start
  6.5 0.7 all-gather.2.cloned.1.call-update
  7.3 0.0 reduce-scatter.2.cloned.1.call-start
  7.3 189.2 %all-gather.2.cloned.1.call-done = bf16[6144,1024]{1,0:T(8,128)(2,1)} async-done(((bf16[96,1024]{1,0:T(8,128)(2,1)}), bf16[6144,1024]{1,0:T(8,128)(2,1)}) %all-gather.2.cloned.1.call-update) | async-done | bytes 12582928 | tf_op jit(solution)/shard_map/all_gather | solution.py:17
  196.5 10.1 %fusion = f32[96,6144]{1,0:T(8,128)} fusion(bf16[96,1024]{1,0:T(8,128)(2,1)} %param.1, bf16[6144,1024]{1,0:T(8,128)(2,1)} %all-gather.2.cloned.1.call-done), kind=kOutput, calls=%fused_computation.4 | convolution fusion | flops 1207959552 | bytes 15138816 | tf_op jit(solution)/shard_map/dot_general | solution.py:8
  206.6 0.0 reduce-scatter.2.cloned.1.call-update
  206.6 1.3 dynamic-slice
  208.5 0.0 copy-done
  208.5 0.1 multiply_reduce_fusion
  208.7 15.0 %psum.7 = f32[96]{0:T(128)S(1)} all-reduce(f32[96]{0:T(128)S(1)} %multiply_reduce_fusion), channel_id=1, replica_groups=mesh['ex'=64,'feat'=8] {'feat'}, use_global_device_ids=true, to_apply=%region_2.0 | all-reduce | flops 96 | bytes 768 | tf_op jit(solution)/shard_map/psum | solution.py:15
  223.7 0.3 dynamic-update-slice
  224.0 254.7 %all-reduce = f32[6144]{0:T(1024)S(1)} all-reduce(f32[6144]{0:T(1024)S(1)} %dynamic-update-slice), channel_id=1, replica_groups=mesh['ex'=64,'feat'=8] {'ex'}, use_global_device_ids=true, to_apply=%add | all-reduce | flops 6144 | bytes 49152
  478.7 0.1 add_rsqrt_fusion
  478.7 0.0 reduce-scatter.2.cloned.1.call-done
  478.7 1.8 multiply_multiply_fusion
  (2 shorter events, 0.0 us)
Async XLA Ops:
  6.5 202.0 %copy-start = (bf16[96,1024]{1,0:T(8,128)(2,1)S(1)}, bf16[96,1024]{1,0:T(8,128)(2,1)}, u32[]{:S(2)}) copy-start(bf16[96,1024]{1,0:T(8,128)(2,1)} %param.1) | copy-start | bytes 589828
  6.5 190.0 %all-gather.2.cloned.1.call-start = ((), (), s32[]{:S(2)}) async-start(), calls=%async_computation.1 | async-start | bytes 12779520 | tf_op jit(solution)/shard_map/all_gather | solution.py:17
  7.3 471.5 %reduce-scatter.2.cloned.1.call-start = ((), (), s32[]{:S(2)}) async-start(), calls=%async_computation.2 | async-start | bytes 2654208 | tf_op jit(solution)/shard_map/reduce_scatter | solution.py:18
Sparse Core Ops, SparseCore 0:
  10.6 185.8 all-gather.1
  206.7 59.9 reduce-scatter.1
where the time goes:
time: 491 us; the launch traced here: 487 us
  blocking collectives  270 us (55%)
  waiting for transfers between devices  190 us (39%)
  between operations  14.1 us (3%)
  matrix products  10.1 us (2%)
    unnamed x1, blocking collectives  255 us
    all_gather x1, waiting for transfers between devices, shards(): lax.all_gather(features, 'ex', axis=0, tiled=True)  189 us
    psum x1, blocking collectives, shards(): row_norms = lax.psum(local_squares, 'feat')  15 us
    dot_general x1, matrix products, inner_tile(): lax.dot_general(left, right, (((1,), (1,)), ((), ())), preferred_element_...  10.1 us
  transfers between devices with their start and end apart: 2, of which 1 were waited for; matrix products, arithmetic and copies ran while one was open for 0% of the time, Pallas kernels for 0%

commit v1 on v0

v1 whole, which is shorter than its diff:
```python
import jax
import jax.numpy as jnp
from jax import lax
from jax.experimental import pallas as pl
from jax.experimental.pallas import tpu as pltpu
from jax.sharding import Mesh, PartitionSpec as P

AXES = ("xh", "z", "co", "yh", "yl", "xl")
SIZES = (2, 16, 2, 2, 2, 2)
ROWS = 96
DEPTH = 1024
PLANES = 16
GROUP = 4
EPS = 1e-06


def wide(left, right):
    return lax.dot_general(left, right, (((1,), (1,)), ((), ())), preferred_element_type=jnp.float32)


def squares_along_lanes(block):
    ones = jnp.ones((8, block.shape[1]), jnp.bfloat16)
    full = block.astype(jnp.float32)
    full = full * full
    high = full.astype(jnp.bfloat16)
    low = (full - high.astype(jnp.float32)).astype(jnp.bfloat16)
    return wide(ones, high) + wide(ones, low)


def partial_kernel(where_ref, *refs):
    rows_in, cols_in = refs[:4], refs[4 : 4 + PLANES]
    out_ref, rows_ref, cols_ref, sems = refs[4 + PLANES :]
    copies = []
    for i, source in enumerate(rows_in):
        at = pl.multiple_of(where_ref[i] * ROWS, ROWS)
        copies.append(pltpu.make_async_copy(source, rows_ref.at[pl.ds(at, ROWS)], sems.at[i]))
    for i, source in enumerate(cols_in):
        at = pl.multiple_of(where_ref[4 + i] * ROWS, ROWS)
        copies.append(pltpu.make_async_copy(source, cols_ref.at[pl.ds(at, ROWS)], sems.at[4 + i]))
    for copy in copies:
        copy.start()
    for copy in copies:
        copy.wait()
    width = GROUP * ROWS
    row_squares = squares_along_lanes(rows_ref[...])
    for group in range(PLANES // GROUP):
        block = cols_ref[group * width : (group + 1) * width]
        gram = wide(rows_ref[...], block)
        col_squares = squares_along_lanes(block)
        for row in range(4):
            slot = row * (PLANES // GROUP) + group
            out_ref[slot, 0:ROWS] = gram[row * ROWS : (row + 1) * ROWS]
            out_ref[slot, ROWS : ROWS + 4] = col_squares[0:4]
            out_ref[slot, ROWS + 4 : ROWS + 8, 0:ROWS] = row_squares[0:4, row * ROWS : (row + 1) * ROWS]


def final_kernel(parts_ref, out_ref):
    def total(core):
        terms = [parts_ref[(xh * 2 + core) * 4 + low] for xh in range(2) for low in range(4)]
        while len(terms) > 1:
            terms = [a + b for a, b in zip(terms[::2], terms[1::2])]
        return terms[0]

    halves = [total(0), total(1)]
    diagonal = lax.broadcasted_iota(jnp.int32, (ROWS, ROWS), 0) == lax.broadcasted_iota(jnp.int32, (ROWS, ROWS), 1)
    along = halves[0][ROWS + 4 : ROWS + 5, 0:ROWS]
    row_squares = jnp.sum(jnp.where(diagonal, along, 0.0), axis=1, keepdims=True)
    row_scale = lax.rsqrt(row_squares + EPS)
    scaled = [half[0:ROWS] * row_scale * lax.rsqrt(half[ROWS : ROWS + 1] + EPS) for half in halves]
    for low in range(GROUP):
        for core in range(2):
            at = (low * 2 + core) * ROWS
            out_ref[:, at : at + ROWS] = scaled[core][:, low * ROWS : (low + 1) * ROWS]


def shards(features):
    xh_yh = [(a, b) for a in range(2) for b in range(2)]
    own = lax.ppermute(features, ("xh", "yh"), [(2 * a + b, 2 * b + a) for a, b in xh_yh])
    upward = [(i, (i + 1) % PLANES) for i in range(PLANES)]
    downward = [(i, (i - 1) % PLANES) for i in range(PLANES)]
    blocks = {0: own}
    up = down = own
    for step in range(1, PLANES // 2 + 1):
        up = lax.ppermute(up, "z", upward)
        blocks[PLANES - step] = up
        if step < PLANES // 2:
            down = lax.ppermute(down, "z", downward)
            blocks[step] = down
    other = lax.ppermute(features, ("xh", "yh"), [(2 * a + b, 2 * b + 1 - a) for a, b in xh_yh])
    swap = [(0, 1), (1, 0)]
    own_across = lax.ppermute(own, "co", swap)
    other_across = lax.ppermute(other, "co", swap)
    yh, co, z = (lax.axis_index(name) for name in ("yh", "co", "z"))
    row_at = [2 * yh + co, 2 * (1 - yh) + co, 2 * yh + 1 - co, 2 * (1 - yh) + 1 - co]
    col_at = [(z + i) % PLANES for i in range(PLANES)]
    where = jnp.stack(row_at + col_at).astype(jnp.int32)
    groups = PLANES // GROUP
    parts = pl.pallas_call(
        partial_kernel,
        out_shape=jax.ShapeDtypeStruct((4 * groups, ROWS + 8, GROUP * ROWS), jnp.float32),
        in_specs=[pl.BlockSpec(memory_space=pltpu.SMEM)] + [pl.BlockSpec(memory_space=pl.ANY)] * (4 + PLANES),
        out_specs=pl.BlockSpec(memory_space=pltpu.VMEM),
        scratch_shapes=[
            pltpu.VMEM((4 * ROWS, DEPTH), jnp.bfloat16),
            pltpu.VMEM((PLANES * ROWS, DEPTH), jnp.bfloat16),
            pltpu.SemaphoreType.DMA((4 + PLANES,)),
        ],
        compiler_params=pltpu.CompilerParams(vmem_limit_bytes=40 << 20),
    )(where, own, other, own_across, other_across, *[blocks[i] for i in range(PLANES)])
    parts = lax.all_to_all(parts, ("xh", "co", "yl", "xl"), 0, 0)
    return pl.pallas_call(
        final_kernel,
        out_shape=jax.ShapeDtypeStruct((ROWS, 2 * GROUP * ROWS), jnp.float32),
        in_specs=[pl.BlockSpec(memory_space=pltpu.VMEM)],
        out_specs=pl.BlockSpec(memory_space=pltpu.VMEM),
        compiler_params=pltpu.CompilerParams(vmem_limit_bytes=40 << 20),
    )(parts)


def solution(mesh):
    split = Mesh(mesh.devices.reshape(SIZES), AXES)
    placed = P(("xh", "z", "co"), ("yh", "yl", "xl"))
    return jax.shard_map(shards, mesh=split, in_specs=(placed,), out_specs=placed, check_vma=False)
```

time: 491 us -> 146 us (0.30)
  blocking collectives: 270 us -> 36.5 us
  waiting for transfers between devices: 190 us -> 14.4 us
  starting transfers between devices: 0.04 us -> 81.9 us
  between operations: 14.1 us -> 0.46 us
  Pallas kernels: 0 us -> 11.4 us
  matrix products: 10.1 us -> 0 us
    unnamed x1 -> x0, blocking collectives: 255 us -> none
    all_gather x1 -> x0, waiting for transfers between devices: 189 us -> none  [shards(): lax.all_gather(features, 'ex', axis=0, tiled=True)]
    ppermute x0 -> x19, starting transfers between devices: none -> 81.9 us  [the longest x7 37.2 us: shards(): down = lax.ppermute(down, 'z', downward)]
    all_to_all x0 -> x1, blocking collectives: none -> 36.5 us  [shards(): parts = lax.all_to_all(parts, ('xh', 'co', 'yl', 'xl'), 0, 0)]
    psum x1 -> x0, blocking collectives: 15 us -> none  [shards(): row_norms = lax.psum(local_squares, 'feat')]
    ppermute x0 -> x19, waiting for transfers between devices: none -> 14.4 us  [the longest x8 12.9 us: shards(): up = lax.ppermute(up, 'z', upward)]
    pallas_call x0 -> x2, Pallas kernels: none -> 11.4 us  [the longest x1 10.4 us: shards(): pl.pallas_call(partial_kernel, out_shape=jax.ShapeDtypeStruct((4 * groups...]
    dot_general x1 -> x0, matrix products: 10.1 us -> none  [inner_tile(): lax.dot_general(left, right, (((1,), (1,)), ((), ())), preferred_element_...]
  transfers between devices with their start and end apart: 2 -> 19, of which waited for: 1 -> 7; matrix products, arithmetic and copies ran while one was open for 0% -> 0% of each run, Pallas kernels for 0% -> 0%
where the time goes in v1:
time: 146 us; the launch traced here: 145 us
  starting transfers between devices  81.9 us (56%)
  blocking collectives  36.5 us (25%)
  waiting for transfers between devices  14.4 us (10%)
  Pallas kernels  11.4 us (8%)
    ppermute x7, starting transfers between devices, shards(): down = lax.ppermute(down, 'z', downward)  37.2 us
    all_to_all x1, blocking collectives, shards(): parts = lax.all_to_all(parts, ('xh', 'co', 'yl', 'xl'), 0, 0)  36.5 us
    ppermute x8, starting transfers between devices, shards(): up = lax.ppermute(up, 'z', upward)  17.8 us
    ppermute x1, starting transfers between devices, shards(): lax.ppermute(features, ('xh', 'yh'), [(2 * a + b, 2 * b + 1 - a) for a, b...  13.4 us
    ppermute x8, waiting for transfers between devices, shards(): up = lax.ppermute(up, 'z', upward)  12.9 us
    pallas_call x1, Pallas kernels, shards(): pl.pallas_call(partial_kernel, out_shape=jax.ShapeDtypeStruct((4 * groups...  10.4 us
    ppermute x1, starting transfers between devices, shards(): own_across = lax.ppermute(own, 'co', swap)  10.1 us
  transfers between devices with their start and end apart: 19, of which 7 were waited for; matrix products, arithmetic and copies ran while one was open for 0% of the time, Pallas kernels for 0%

profile of v1, /device:TPU:1, one launch (start us, length us, event | category | flops | bytes accessed | tf_op | source)
XLA Modules:
  0.0 144.8 jit_solution(13679794889852409902)
XLA Ops:
  0.0 1.6 %collective-permute-start = (bf16[96,1024]{1,0:T(8,128)(2,1)}, bf16[96,1024]{1,0:T(8,128)(2,1)S(1)}, u32[]{:S(2)}, u32[]{:S(2)}) collective-permute-start(bf16[96,1024]{1,0:T(8,128)(2,1)} %param.1), channel_id=1, source_target_pairs={{0,0},{4,256},{256,4},{260,260},{1,1},{5,257},{257,5},{261,261},{2... | collective-permute-start | bytes 589832 | tf_op jit(solution)/shard_map/ppermute | solution.py:78
  1.6 4.4 %collective-permute-start.11 = (bf16[96,1024]{1,0:T(8,128)(2,1)S(1)}, bf16[96,1024]{1,0:T(8,128)(2,1)S(1)}, u32[]{:S(2)}, u32[]{:S(2)}) collective-permute-start(bf16[96,1024]{1,0:T(8,128)(2,1)S(1)} %collective-permute-done.refs_0_.refs_4_), channel_id=1, source_target_pairs={{0,16},{16,32},{32,48},{48,64},{64,80},{80,96},{96,112},{112,128},... | collective-permute-start | bytes 589832 | tf_op jit(solution)/shard_map/ppermute | solution.py:84
  5.9 9.5 %collective-permute-start.4 = (bf16[96,1024]{1,0:T(8,128)(2,1)S(1)}, bf16[96,1024]{1,0:T(8,128)(2,1)S(1)}, u32[]{:S(2)}, u32[]{:S(2)}) collective-permute-start(bf16[96,1024]{1,0:T(8,128)(2,1)S(1)} %collective-permute-done.refs_0_.refs_4_), channel_id=1, source_target_pairs={{0,240},{16,0},{32,16},{48,32},{64,48},{80,64},{96,80},{112,96},{1... | collective-permute-start | bytes 589832 | tf_op jit(solution)/shard_map/ppermute | solution.py:87
  15.5 2.7 %collective-permute-done.11.refs_19_ = bf16[96,1024]{1,0:T(8,128)(2,1)S(1)} collective-permute-done((bf16[96,1024]{1,0:T(8,128)(2,1)S(1)}, bf16[96,1024]{1,0:T(8,128)(2,1)S(1)}, u32[]{:S(2)}, u32[]{:S(2)}) %collective-permute-start.11) | collective-permute-done | bytes 196640 | tf_op jit(solution)/shard_map/ppermute | solution.py:84
  18.1 1.9 %collective-permute-start.12 = (bf16[96,1024]{1,0:T(8,128)(2,1)S(1)}, bf16[96,1024]{1,0:T(8,128)(2,1)S(1)}, u32[]{:S(2)}, u32[]{:S(2)}) collective-permute-start(bf16[96,1024]{1,0:T(8,128)(2,1)S(1)} %collective-permute-done.11.refs_19_), channel_id=1, source_target_pairs={{0,16},{16,32},{32,48},{48,64},{64,80},{80,96},{96,112},{112,128},... | collective-permute-start | bytes 589832 | tf_op jit(solution)/shard_map/ppermute | solution.py:84
  20.1 4.6 %collective-permute-start.5 = (bf16[96,1024]{1,0:T(8,128)(2,1)S(1)}, bf16[96,1024]{1,0:T(8,128)(2,1)S(1)}, u32[]{:S(2)}, u32[]{:S(2)}) collective-permute-start(bf16[96,1024]{1,0:T(8,128)(2,1)S(1)} %collective-permute-done.4.refs_5_), channel_id=1, source_target_pairs={{0,240},{16,0},{32,16},{48,32},{64,48},{80,64},{96,80},{112,96},{1... | collective-permute-start | bytes 589832 | tf_op jit(solution)/shard_map/ppermute | solution.py:87
  24.6 1.8 %collective-permute-done.12.refs_18_ = bf16[96,1024]{1,0:T(8,128)(2,1)S(1)} collective-permute-done((bf16[96,1024]{1,0:T(8,128)(2,1)S(1)}, bf16[96,1024]{1,0:T(8,128)(2,1)S(1)}, u32[]{:S(2)}, u32[]{:S(2)}) %collective-permute-start.12) | collective-permute-done | bytes 196640 | tf_op jit(solution)/shard_map/ppermute | solution.py:84
  26.4 1.9 %collective-permute-start.13 = (bf16[96,1024]{1,0:T(8,128)(2,1)S(1)}, bf16[96,1024]{1,0:T(8,128)(2,1)S(1)}, u32[]{:S(2)}, u32[]{:S(2)}) collective-permute-start(bf16[96,1024]{1,0:T(8,128)(2,1)S(1)} %collective-permute-done.12.refs_18_), channel_id=1, source_target_pairs={{0,16},{16,32},{32,48},{48,64},{64,80},{80,96},{96,112},{112,128},... | collective-permute-start | bytes 589832 | tf_op jit(solution)/shard_map/ppermute | solution.py:84
  28.3 0.0 collective-permute-done.5.refs_6_
  28.3 4.6 %collective-permute-start.6 = (bf16[96,1024]{1,0:T(8,128)(2,1)S(1)}, bf16[96,1024]{1,0:T(8,128)(2,1)S(1)}, u32[]{:S(2)}, u32[]{:S(2)}) collective-permute-start(bf16[96,1024]{1,0:T(8,128)(2,1)S(1)} %collective-permute-done.5.refs_6_), channel_id=1, source_target_pairs={{0,240},{16,0},{32,16},{48,32},{64,48},{80,64},{96,80},{112,96},{1... | collective-permute-start | bytes 589832 | tf_op jit(solution)/shard_map/ppermute | solution.py:87
  32.9 1.1 collective-permute-done.13.refs_17_
  34.0 1.9 %collective-permute-start.14 = (bf16[96,1024]{1,0:T(8,128)(2,1)S(1)}, bf16[96,1024]{1,0:T(8,128)(2,1)S(1)}, u32[]{:S(2)}, u32[]{:S(2)}) collective-permute-start(bf16[96,1024]{1,0:T(8,128)(2,1)S(1)} %collective-permute-done.13.refs_17_), channel_id=1, source_target_pairs={{0,16},{16,32},{32,48},{48,64},{64,80},{80,96},{96,112},{112,128},... | collective-permute-start | bytes 589832 | tf_op jit(solution)/shard_map/ppermute | solution.py:84
  35.9 0.0 collective-permute-done.6.refs_7_
  35.9 4.6 %collective-permute-start.7 = (bf16[96,1024]{1,0:T(8,128)(2,1)S(1)}, bf16[96,1024]{1,0:T(8,128)(2,1)S(1)}, u32[]{:S(2)}, u32[]{:S(2)}) collective-permute-start(bf16[96,1024]{1,0:T(8,128)(2,1)S(1)} %collective-permute-done.6.refs_7_), channel_id=1, source_target_pairs={{0,240},{16,0},{32,16},{48,32},{64,48},{80,64},{96,80},{112,96},{1... | collective-permute-start | bytes 589832 | tf_op jit(solution)/shard_map/ppermute | solution.py:87
  40.5 1.1 collective-permute-done.14.refs_16_
  41.6 1.9 %collective-permute-start.15 = (bf16[96,1024]{1,0:T(8,128)(2,1)S(1)}, bf16[96,1024]{1,0:T(8,128)(2,1)S(1)}, u32[]{:S(2)}, u32[]{:S(2)}) collective-permute-start(bf16[96,1024]{1,0:T(8,128)(2,1)S(1)} %collective-permute-done.14.refs_16_), channel_id=1, source_target_pairs={{0,16},{16,32},{32,48},{48,64},{64,80},{80,96},{96,112},{112,128},... | collective-permute-start | bytes 589832 | tf_op jit(solution)/shard_map/ppermute | solution.py:84
  43.6 4.6 %collective-permute-start.8 = (bf16[96,1024]{1,0:T(8,128)(2,1)S(1)}, bf16[96,1024]{1,0:T(8,128)(2,1)S(1)}, u32[]{:S(2)}, u32[]{:S(2)}) collective-permute-start(bf16[96,1024]{1,0:T(8,128)(2,1)S(1)} %collective-permute-done.7.refs_8_), channel_id=1, source_target_pairs={{0,240},{16,0},{32,16},{48,32},{64,48},{80,64},{96,80},{112,96},{1... | collective-permute-start | bytes 589832 | tf_op jit(solution)/shard_map/ppermute | solution.py:87
  48.1 1.1 collective-permute-done.15.refs_15_
  49.2 1.9 %collective-permute-start.16 = (bf16[96,1024]{1,0:T(8,128)(2,1)S(1)}, bf16[96,1024]{1,0:T(8,128)(2,1)S(1)}, u32[]{:S(2)}, u32[]{:S(2)}) collective-permute-start(bf16[96,1024]{1,0:T(8,128)(2,1)S(1)} %collective-permute-done.15.refs_15_), channel_id=1, source_target_pairs={{0,16},{16,32},{32,48},{48,64},{64,80},{80,96},{96,112},{112,128},... | collective-permute-start | bytes 589832 | tf_op jit(solution)/shard_map/ppermute | solution.py:84
  51.2 13.4 %collective-permute-start.1 = (bf16[96,1024]{1,0:T(8,128)(2,1)}, bf16[96,1024]{1,0:T(8,128)(2,1)S(1)}, u32[]{:S(2)}, u32[]{:S(2)}) collective-permute-start(bf16[96,1024]{1,0:T(8,128)(2,1)} %param.1), channel_id=1, source_target_pairs={{0,4},{4,260},{256,0},{260,256},{1,5},{5,261},{257,1},{261,257},{2... | collective-permute-start | bytes 589832 | tf_op jit(solution)/shard_map/ppermute | solution.py:89
  64.6 4.6 %collective-permute-start.9 = (bf16[96,1024]{1,0:T(8,128)(2,1)S(1)}, bf16[96,1024]{1,0:T(8,128)(2,1)S(1)}, u32[]{:S(2)}, u32[]{:S(2)}) collective-permute-start(bf16[96,1024]{1,0:T(8,128)(2,1)S(1)} %collective-permute-done.8.refs_9_), channel_id=1, source_target_pairs={{0,240},{16,0},{32,16},{48,32},{64,48},{80,64},{96,80},{112,96},{1... | collective-permute-start | bytes 589832 | tf_op jit(solution)/shard_map/ppermute | solution.py:87
  69.2 1.9 %collective-permute-start.17 = (bf16[96,1024]{1,0:T(8,128)(2,1)S(1)}, bf16[96,1024]{1,0:T(8,128)(2,1)S(1)}, u32[]{:S(2)}, u32[]{:S(2)}) collective-permute-start(bf16[96,1024]{1,0:T(8,128)(2,1)S(1)} %collective-permute-done.16.refs_14_), channel_id=1, source_target_pairs={{0,16},{16,32},{32,48},{48,64},{64,80},{80,96},{96,112},{112,128},... | collective-permute-start | bytes 589832 | tf_op jit(solution)/shard_map/ppermute | solution.py:84
  71.1 10.1 %collective-permute-start.2 = (bf16[96,1024]{1,0:T(8,128)(2,1)S(1)}, bf16[96,1024]{1,0:T(8,128)(2,1)S(1)}, u32[]{:S(2)}, u32[]{:S(2)}) collective-permute-start(bf16[96,1024]{1,0:T(8,128)(2,1)S(1)} %collective-permute-done.refs_0_.refs_4_), channel_id=1, source_target_pairs={{0,8},{8,0},{1,9},{9,1},{2,10},{10,2},{3,11},{11,3},{4,12},{12,4},... | collective-permute-start | bytes 589832 | tf_op jit(solution)/shard_map/ppermute | solution.py:91
  81.2 1.9 %collective-permute-start.3 = (bf16[96,1024]{1,0:T(8,128)(2,1)S(1)}, bf16[96,1024]{1,0:T(8,128)(2,1)S(1)}, u32[]{:S(2)}, u32[]{:S(2)}) collective-permute-start(bf16[96,1024]{1,0:T(8,128)(2,1)S(1)} %collective-permute-done.1.refs_1_), channel_id=1, source_target_pairs={{0,8},{8,0},{1,9},{9,1},{2,10},{10,2},{3,11},{11,3},{4,12},{12,4},... | collective-permute-start | bytes 589832 | tf_op jit(solution)/shard_map/ppermute | solution.py:92
  83.1 4.9 %collective-permute-start.10 = (bf16[96,1024]{1,0:T(8,128)(2,1)S(1)}, bf16[96,1024]{1,0:T(8,128)(2,1)S(1)}, u32[]{:S(2)}, u32[]{:S(2)}) collective-permute-start(bf16[96,1024]{1,0:T(8,128)(2,1)S(1)} %collective-permute-done.9.refs_10_), channel_id=1, source_target_pairs={{0,240},{16,0},{32,16},{48,32},{64,48},{80,64},{96,80},{112,96},{1... | collective-permute-start | bytes 589832 | tf_op jit(solution)/shard_map/ppermute | solution.py:87
  88.0 1.9 %collective-permute-start.18 = (bf16[96,1024]{1,0:T(8,128)(2,1)S(1)}, bf16[96,1024]{1,0:T(8,128)(2,1)}, u32[]{:S(2)}, u32[]{:S(2)}) collective-permute-start(bf16[96,1024]{1,0:T(8,128)(2,1)S(1)} %collective-permute-done.17.refs_13_), channel_id=1, source_target_pairs={{0,16},{16,32},{32,48},{48,64},{64,80},{80,96},{96,112},{112,128},... | collective-permute-start | bytes 589832 | tf_op jit(solution)/shard_map/ppermute | solution.py:84
  90.1 0.1 stack.83.where_ref
  90.3 1.5 %collective-permute-done.10.refs_11_ = bf16[96,1024]{1,0:T(8,128)(2,1)S(1)} collective-permute-done((bf16[96,1024]{1,0:T(8,128)(2,1)S(1)}, bf16[96,1024]{1,0:T(8,128)(2,1)S(1)}, u32[]{:S(2)}, u32[]{:S(2)}) %collective-permute-start.10) | collective-permute-done | bytes 196640 | tf_op jit(solution)/shard_map/ppermute | solution.py:87
  91.7 5.1 %collective-permute-done.18.refs_12_ = bf16[96,1024]{1,0:T(8,128)(2,1)} collective-permute-done((bf16[96,1024]{1,0:T(8,128)(2,1)S(1)}, bf16[96,1024]{1,0:T(8,128)(2,1)}, u32[]{:S(2)}, u32[]{:S(2)}) %collective-permute-start.18) | collective-permute-done | bytes 196640 | tf_op jit(solution)/shard_map/ppermute | solution.py:84
  96.8 10.4 %shard_map.17 = f32[16,104,384]{2,1,0:T(8,128)S(1)} custom-call(s32[20]{0:T(128)S(1)} %stack.83.where_ref, bf16[96,1024]{1,0:T(8,128)(2,1)S(1)} %collective-permute-done.refs_0_.refs_4_, bf16[96,1024]{1,0:T(8,128)(2,1)S(1)} %collective-permute-done.1.refs_1_, bf16[96,1024]{1,0:T(8,128)(2,1)S(1)} %collective-permute-done.2.refs_2_, ...), custom_call_target="tpu_custom_call" | custom-call | tf_op jit(solution)/shard_map/pallas_call | solution.py:98
  107.3 36.5 %all_to_all.5.parts_ref = f32[16,104,384]{2,1,0:T(8,128)S(1)} all-to-all(f32[16,104,384]{2,1,0:T(8,128)S(1)} %shard_map.17), channel_id=1, replica_groups=mesh['xh'=2,'z'=16,'co'=2,'yh'=2,'yl'=2,'xl'=2] {'xh','co','yl','xl'}, dimensions={0} | all-to-all | bytes 5111808 | tf_op jit(solution)/shard_map/all_to_all | solution.py:110
  143.8 1.0 shard_map.18
  (10 shorter events, 0.0 us)
Async XLA Ops:
  0.0 1.6 %collective-permute-start = (bf16[96,1024]{1,0:T(8,128)(2,1)}, bf16[96,1024]{1,0:T(8,128)(2,1)S(1)}, u32[]{:S(2)}, u32[]{:S(2)}) collective-permute-start(bf16[96,1024]{1,0:T(8,128)(2,1)} %param.1), channel_id=1, source_target_pairs={{0,0},{4,256},{256,4},{260,260},{1,1},{5,257},{257,5},{261,261},{2... | collective-permute-start | bytes 589832 | tf_op jit(solution)/shard_map/ppermute | solution.py:78
  1.6 16.6 %collective-permute-start.11 = (bf16[96,1024]{1,0:T(8,128)(2,1)S(1)}, bf16[96,1024]{1,0:T(8,128)(2,1)S(1)}, u32[]{:S(2)}, u32[]{:S(2)}) collective-permute-start(bf16[96,1024]{1,0:T(8,128)(2,1)S(1)} %collective-permute-done.refs_0_.refs_4_), channel_id=1, source_target_pairs={{0,16},{16,32},{32,48},{48,64},{64,80},{80,96},{96,112},{112,128},... | collective-permute-start | bytes 589832 | tf_op jit(solution)/shard_map/ppermute | solution.py:84
  5.9 14.1 %collective-permute-start.4 = (bf16[96,1024]{1,0:T(8,128)(2,1)S(1)}, bf16[96,1024]{1,0:T(8,128)(2,1)S(1)}, u32[]{:S(2)}, u32[]{:S(2)}) collective-permute-start(bf16[96,1024]{1,0:T(8,128)(2,1)S(1)} %collective-permute-done.refs_0_.refs_4_), channel_id=1, source_target_pairs={{0,240},{16,0},{32,16},{48,32},{64,48},{80,64},{96,80},{112,96},{1... | collective-permute-start | bytes 589832 | tf_op jit(solution)/shard_map/ppermute | solution.py:87
  18.1 8.3 %collective-permute-start.12 = (bf16[96,1024]{1,0:T(8,128)(2,1)S(1)}, bf16[96,1024]{1,0:T(8,128)(2,1)S(1)}, u32[]{:S(2)}, u32[]{:S(2)}) collective-permute-start(bf16[96,1024]{1,0:T(8,128)(2,1)S(1)} %collective-permute-done.11.refs_19_), channel_id=1, source_target_pairs={{0,16},{16,32},{32,48},{48,64},{64,80},{80,96},{96,112},{112,128},... | collective-permute-start | bytes 589832 | tf_op jit(solution)/shard_map/ppermute | solution.py:84
  20.1 8.3 %collective-permute-start.5 = (bf16[96,1024]{1,0:T(8,128)(2,1)S(1)}, bf16[96,1024]{1,0:T(8,128)(2,1)S(1)}, u32[]{:S(2)}, u32[]{:S(2)}) collective-permute-start(bf16[96,1024]{1,0:T(8,128)(2,1)S(1)} %collective-permute-done.4.refs_5_), channel_id=1, source_target_pairs={{0,240},{16,0},{32,16},{48,32},{64,48},{80,64},{96,80},{112,96},{1... | collective-permute-start | bytes 589832 | tf_op jit(solution)/shard_map/ppermute | solution.py:87
  26.4 7.6 %collective-permute-start.13 = (bf16[96,1024]{1,0:T(8,128)(2,1)S(1)}, bf16[96,1024]{1,0:T(8,128)(2,1)S(1)}, u32[]{:S(2)}, u32[]{:S(2)}) collective-permute-start(bf16[96,1024]{1,0:T(8,128)(2,1)S(1)} %collective-permute-done.12.refs_18_), channel_id=1, source_target_pairs={{0,16},{16,32},{32,48},{48,64},{64,80},{80,96},{96,112},{112,128},... | collective-permute-start | bytes 589832 | tf_op jit(solution)/shard_map/ppermute | solution.py:84
  28.3 7.6 %collective-permute-start.6 = (bf16[96,1024]{1,0:T(8,128)(2,1)S(1)}, bf16[96,1024]{1,0:T(8,128)(2,1)S(1)}, u32[]{:S(2)}, u32[]{:S(2)}) collective-permute-start(bf16[96,1024]{1,0:T(8,128)(2,1)S(1)} %collective-permute-done.5.refs_6_), channel_id=1, source_target_pairs={{0,240},{16,0},{32,16},{48,32},{64,48},{80,64},{96,80},{112,96},{1... | collective-permute-start | bytes 589832 | tf_op jit(solution)/shard_map/ppermute | solution.py:87
  34.0 7.6 %collective-permute-start.14 = (bf16[96,1024]{1,0:T(8,128)(2,1)S(1)}, bf16[96,1024]{1,0:T(8,128)(2,1)S(1)}, u32[]{:S(2)}, u32[]{:S(2)}) collective-permute-start(bf16[96,1024]{1,0:T(8,128)(2,1)S(1)} %collective-permute-done.13.refs_17_), channel_id=1, source_target_pairs={{0,16},{16,32},{32,48},{48,64},{64,80},{80,96},{96,112},{112,128},... | collective-permute-start | bytes 589832 | tf_op jit(solution)/shard_map/ppermute | solution.py:84
  35.9 7.6 %collective-permute-start.7 = (bf16[96,1024]{1,0:T(8,128)(2,1)S(1)}, bf16[96,1024]{1,0:T(8,128)(2,1)S(1)}, u32[]{:S(2)}, u32[]{:S(2)}) collective-permute-start(bf16[96,1024]{1,0:T(8,128)(2,1)S(1)} %collective-permute-done.6.refs_7_), channel_id=1, source_target_pairs={{0,240},{16,0},{32,16},{48,32},{64,48},{80,64},{96,80},{112,96},{1... | collective-permute-start | bytes 589832 | tf_op jit(solution)/shard_map/ppermute | solution.py:87
  41.6 7.6 %collective-permute-start.15 = (bf16[96,1024]{1,0:T(8,128)(2,1)S(1)}, bf16[96,1024]{1,0:T(8,128)(2,1)S(1)}, u32[]{:S(2)}, u32[]{:S(2)}) collective-permute-start(bf16[96,1024]{1,0:T(8,128)(2,1)S(1)} %collective-permute-done.14.refs_16_), channel_id=1, source_target_pairs={{0,16},{16,32},{32,48},{48,64},{64,80},{80,96},{96,112},{112,128},... | collective-permute-start | bytes 589832 | tf_op jit(solution)/shard_map/ppermute | solution.py:84
  43.6 21.0 %collective-permute-start.8 = (bf16[96,1024]{1,0:T(8,128)(2,1)S(1)}, bf16[96,1024]{1,0:T(8,128)(2,1)S(1)}, u32[]{:S(2)}, u32[]{:S(2)}) collective-permute-start(bf16[96,1024]{1,0:T(8,128)(2,1)S(1)} %collective-permute-done.7.refs_8_), channel_id=1, source_target_pairs={{0,240},{16,0},{32,16},{48,32},{64,48},{80,64},{96,80},{112,96},{1... | collective-permute-start | bytes 589832 | tf_op jit(solution)/shard_map/ppermute | solution.py:87
  49.2 19.9 %collective-permute-start.16 = (bf16[96,1024]{1,0:T(8,128)(2,1)S(1)}, bf16[96,1024]{1,0:T(8,128)(2,1)S(1)}, u32[]{:S(2)}, u32[]{:S(2)}) collective-permute-start(bf16[96,1024]{1,0:T(8,128)(2,1)S(1)} %collective-permute-done.15.refs_15_), channel_id=1, source_target_pairs={{0,16},{16,32},{32,48},{48,64},{64,80},{80,96},{96,112},{112,128},... | collective-permute-start | bytes 589832 | tf_op jit(solution)/shard_map/ppermute | solution.py:84
  51.2 30.0 %collective-permute-start.1 = (bf16[96,1024]{1,0:T(8,128)(2,1)}, bf16[96,1024]{1,0:T(8,128)(2,1)S(1)}, u32[]{:S(2)}, u32[]{:S(2)}) collective-permute-start(bf16[96,1024]{1,0:T(8,128)(2,1)} %param.1), channel_id=1, source_target_pairs={{0,4},{4,260},{256,0},{260,256},{1,5},{5,261},{257,1},{261,257},{2... | collective-permute-start | bytes 589832 | tf_op jit(solution)/shard_map/ppermute | solution.py:89
  64.6 18.5 %collective-permute-start.9 = (bf16[96,1024]{1,0:T(8,128)(2,1)S(1)}, bf16[96,1024]{1,0:T(8,128)(2,1)S(1)}, u32[]{:S(2)}, u32[]{:S(2)}) collective-permute-start(bf16[96,1024]{1,0:T(8,128)(2,1)S(1)} %collective-permute-done.8.refs_9_), channel_id=1, source_target_pairs={{0,240},{16,0},{32,16},{48,32},{64,48},{80,64},{96,80},{112,96},{1... | collective-permute-start | bytes 589832 | tf_op jit(solution)/shard_map/ppermute | solution.py:87
  69.2 18.8 %collective-permute-start.17 = (bf16[96,1024]{1,0:T(8,128)(2,1)S(1)}, bf16[96,1024]{1,0:T(8,128)(2,1)S(1)}, u32[]{:S(2)}, u32[]{:S(2)}) collective-permute-start(bf16[96,1024]{1,0:T(8,128)(2,1)S(1)} %collective-permute-done.16.refs_14_), channel_id=1, source_target_pairs={{0,16},{16,32},{32,48},{48,64},{64,80},{80,96},{96,112},{112,128},... | collective-permute-start | bytes 589832 | tf_op jit(solution)/shard_map/ppermute | solution.py:84
  71.1 19.1 %collective-permute-start.2 = (bf16[96,1024]{1,0:T(8,128)(2,1)S(1)}, bf16[96,1024]{1,0:T(8,128)(2,1)S(1)}, u32[]{:S(2)}, u32[]{:S(2)}) collective-permute-start(bf16[96,1024]{1,0:T(8,128)(2,1)S(1)} %collective-permute-done.refs_0_.refs_4_), channel_id=1, source_target_pairs={{0,8},{8,0},{1,9},{9,1},{2,10},{10,2},{3,11},{11,3},{4,12},{12,4},... | collective-permute-start | bytes 589832 | tf_op jit(solution)/shard_map/ppermute | solution.py:91
  81.2 9.1 %collective-permute-start.3 = (bf16[96,1024]{1,0:T(8,128)(2,1)S(1)}, bf16[96,1024]{1,0:T(8,128)(2,1)S(1)}, u32[]{:S(2)}, u32[]{:S(2)}) collective-permute-start(bf16[96,1024]{1,0:T(8,128)(2,1)S(1)} %collective-permute-done.1.refs_1_), channel_id=1, source_target_pairs={{0,8},{8,0},{1,9},{9,1},{2,10},{10,2},{3,11},{11,3},{4,12},{12,4},... | collective-permute-start | bytes 589832 | tf_op jit(solution)/shard_map/ppermute | solution.py:92
  83.1 8.6 %collective-permute-start.10 = (bf16[96,1024]{1,0:T(8,128)(2,1)S(1)}, bf16[96,1024]{1,0:T(8,128)(2,1)S(1)}, u32[]{:S(2)}, u32[]{:S(2)}) collective-permute-start(bf16[96,1024]{1,0:T(8,128)(2,1)S(1)} %collective-permute-done.9.refs_10_), channel_id=1, source_target_pairs={{0,240},{16,0},{32,16},{48,32},{64,48},{80,64},{96,80},{112,96},{1... | collective-permute-start | bytes 589832 | tf_op jit(solution)/shard_map/ppermute | solution.py:87
  88.0 8.9 %collective-permute-start.18 = (bf16[96,1024]{1,0:T(8,128)(2,1)S(1)}, bf16[96,1024]{1,0:T(8,128)(2,1)}, u32[]{:S(2)}, u32[]{:S(2)}) collective-permute-start(bf16[96,1024]{1,0:T(8,128)(2,1)S(1)} %collective-permute-done.17.refs_13_), channel_id=1, source_target_pairs={{0,16},{16,32},{32,48},{48,64},{64,80},{80,96},{96,112},{112,128},... | collective-permute-start | bytes 589832 | tf_op jit(solution)/shard_map/ppermute | solution.py:84

commit v2 on v0

v2 whole, which is shorter than its diff:
```python
import jax
import jax.numpy as jnp
from jax import lax
from jax.experimental import pallas as pl
from jax.experimental.pallas import tpu as pltpu
from jax.sharding import Mesh, PartitionSpec as P

AXES = ("xh", "z", "co", "yh", "yl", "xl")
SIZES = (2, 16, 2, 2, 2, 2)
ROWS = 96
TALL = 112
DEPTH = 1024
PLANES = 16
GROUP = 4
EPS = 1e-06
LANES = 128
TOP = 16384.0
FIRST_EXPONENT = 7
NORM_UNIT = 32.0
LIFT = 16384.0


def wide(left, right):
    return lax.dot_general(left, right, (((1,), (1,)), ((), ())), preferred_element_type=jnp.float32)


def on_diagonal(rows, lanes):
    return lax.broadcasted_iota(jnp.int32, (rows, lanes), 0) == lax.broadcasted_iota(jnp.int32, (rows, lanes), 1)


def scale_kernel(x_ref, out_ref):
    values = x_ref[...].astype(jnp.float32)
    largest = jnp.max(jnp.max(jnp.abs(values), axis=1, keepdims=True), axis=0, keepdims=True)
    scale = jnp.full((1, 1), 2.0**FIRST_EXPONENT, jnp.float32)
    exponent = jnp.full((1, 1), float(FIRST_EXPONENT), jnp.float32)
    for bit in (32, 16, 8, 4, 2, 1):
        fits = largest * scale * 2.0**bit < TOP
        scale = jnp.where(fits, scale * 2.0**bit, scale)
        exponent = jnp.where(fits, exponent + bit, exponent)
    scaled = values * scale
    out_ref[0:ROWS] = scaled.astype(jnp.bfloat16)
    norms = jnp.sqrt(jnp.sum(scaled * scaled, axis=1, keepdims=True)) * (1.0 / NORM_UNIT)
    along = jnp.sum(jnp.where(on_diagonal(ROWS, LANES), norms, 0.0), axis=0, keepdims=True)

    def rounded(x):
        return x.astype(jnp.bfloat16).astype(jnp.float32)

    high = rounded(along)
    middle = rounded((along - high) * 256.0)
    low = rounded((along - high - middle * (1.0 / 256.0)) * 65536.0)
    row = lax.broadcasted_iota(jnp.int32, (TALL - ROWS, LANES), 0)
    info = jnp.where(row == 0, high, jnp.where(row == 1, middle, jnp.where(row == 2, low, exponent)))
    out_ref[ROWS:TALL] = jnp.zeros((TALL - ROWS, DEPTH), jnp.bfloat16)
    out_ref[ROWS:TALL, 0:LANES] = jnp.where(row < 4, info, 0.0).astype(jnp.bfloat16)


def norm_of(info):
    return (info[0:1] + info[1:2] * (1.0 / 256.0) + info[2:3] * (1.0 / 65536.0)) * NORM_UNIT


def inverse(norm):
    return jnp.where(norm > 0.0, 1.0 / jnp.where(norm > 0.0, norm, 1.0), 0.0)


def partial_kernel(where_ref, *refs):
    rows_in, cols_ref = refs[:4], refs[4]
    out_ref, rows_ref, scale_ref, info_ref = refs[5:]
    groups = PLANES // GROUP
    width = GROUP * ROWS
    diagonal = on_diagonal(ROWS, LANES)
    for i, source in enumerate(rows_in):
        at = pl.multiple_of(where_ref[i] * ROWS, ROWS)
        rows_ref[pl.ds(at, ROWS)] = source[0:ROWS]
        info = source[ROWS:TALL, 0:LANES].astype(jnp.float32)
        down = jnp.sum(jnp.where(diagonal, inverse(norm_of(info)) * LIFT, 0.0), axis=1, keepdims=True)
        scale_ref[pl.ds(at, ROWS)] = jnp.broadcast_to(down, (ROWS, LANES))
        for group in range(groups):
            out_ref[where_ref[i] * groups + group, ROWS + 4 : ROWS + 8, 0:LANES] = info[0:4]
    for group in range(groups):
        for low in range(GROUP):
            start = (group * GROUP + low) * TALL
            info = cols_ref[start + ROWS : start + TALL, 0:LANES].astype(jnp.float32)
            info_ref[0:4, low * ROWS : (low + 1) * ROWS] = info[0:4, 0:ROWS]
        starts = [(group * GROUP + low) * TALL for low in range(GROUP)]
        block = jnp.concatenate([cols_ref[start : start + ROWS] for start in starts], axis=0)
        info = info_ref[0:4]
        across = inverse(norm_of(info))
        gram = wide(rows_ref[...], block)
        for row in range(4):
            slot = row * groups + group
            down = scale_ref[row * ROWS : (row + 1) * ROWS, 0:1]
            out_ref[slot, 0:ROWS] = gram[row * ROWS : (row + 1) * ROWS] * down * across
            out_ref[slot, ROWS : ROWS + 4] = info


def final_kernel(parts_ref, out_ref):
    diagonal = on_diagonal(ROWS, LANES)
    slots = [[(xh * 2 + core) * 4 + low for xh in range(2) for low in range(4)] for core in range(2)]

    def true_norms(core, first, lanes):
        infos = [parts_ref[slot, first : first + 4, 0:lanes] for slot in slots[core]]
        return [norm_of(info) * jnp.exp2(-info[3:4]) for info in infos]

    def weights(norms):
        total = norms[0] * norms[0]
        for norm in norms[1:]:
            total += norm * norm
        shrink = lax.rsqrt(total + EPS) * LIFT**-0.5
        return [norm * shrink for norm in norms]

    rows = weights(true_norms(0, ROWS + 4, LANES))
    rows = [jnp.sum(jnp.where(diagonal, along, 0.0), axis=1, keepdims=True) for along in rows]
    for core in range(2):
        cols = weights(true_norms(core, ROWS, GROUP * ROWS))
        total = jnp.zeros((ROWS, GROUP * ROWS), jnp.float32)
        for slot, down, across in zip(slots[core], rows, cols):
            total += parts_ref[slot, 0:ROWS] * down * across
        for low in range(GROUP):
            at = (low * 2 + core) * ROWS
            out_ref[:, at : at + ROWS] = total[:, low * ROWS : (low + 1) * ROWS]


def shards(features):
    in_vmem = pl.BlockSpec(memory_space=pltpu.VMEM)
    params = pltpu.CompilerParams(vmem_limit_bytes=40 << 20)
    scaled = pl.pallas_call(
        scale_kernel,
        out_shape=jax.ShapeDtypeStruct((TALL, DEPTH), jnp.bfloat16),
        in_specs=[in_vmem],
        out_specs=in_vmem,
        compiler_params=params,
    )(features)
    pairs = [(a, b) for a in range(2) for b in range(2)]
    to_own = [(2 * a + b, 2 * b + a) for a, b in pairs]
    to_other = [(2 * a + b, 2 * b + 1 - a) for a, b in pairs]
    own = lax.ppermute(scaled, ("xh", "yh"), to_own)
    across = lax.ppermute(scaled, "co", [(0, 1), (1, 0)])
    other = lax.ppermute(scaled, ("xh", "yh"), to_other)
    own_across = lax.ppermute(across, ("xh", "yh"), to_own)
    other_across = lax.ppermute(across, ("xh", "yh"), to_other)
    columns = lax.all_gather(own.astype(jnp.float16), "z", axis=0, tiled=True).astype(jnp.bfloat16)
    yh, co = lax.axis_index("yh"), lax.axis_index("co")
    where = jnp.stack([2 * yh + co, 2 * (1 - yh) + co, 2 * yh + 1 - co, 2 * (1 - yh) + 1 - co]).astype(jnp.int32)
    groups = PLANES // GROUP
    parts = pl.pallas_call(
        partial_kernel,
        out_shape=jax.ShapeDtypeStruct((4 * groups, ROWS + 8, GROUP * ROWS), jnp.float32),
        in_specs=[pl.BlockSpec(memory_space=pltpu.SMEM)] + [in_vmem] * 5,
        out_specs=in_vmem,
        scratch_shapes=[
            pltpu.VMEM((4 * ROWS, DEPTH), jnp.bfloat16),
            pltpu.VMEM((4 * ROWS, LANES), jnp.float32),
            pltpu.VMEM((8, GROUP * ROWS), jnp.float32),
        ],
        compiler_params=params,
    )(where, own, other, own_across, other_across, columns)
    parts = lax.all_to_all(parts.astype(jnp.float16), ("xh", "co", "yl", "xl"), 0, 0)
    return pl.pallas_call(
        final_kernel,
        out_shape=jax.ShapeDtypeStruct((ROWS, 2 * GROUP * ROWS), jnp.float32),
        in_specs=[in_vmem],
        out_specs=in_vmem,
        compiler_params=params,
    )(parts.astype(jnp.float32))


def solution(mesh):
    split = Mesh(mesh.devices.reshape(SIZES), AXES)
    placed = P(("xh", "z", "co"), ("yh", "yl", "xl"))
    return jax.shard_map(shards, mesh=split, in_specs=(placed,), out_specs=placed, check_vma=False)
```

time: 491 us -> 112 us (0.23)
  waiting for transfers between devices: 190 us -> 0.01 us
  blocking collectives: 270 us -> 84.4 us
  starting transfers between devices: 0.04 us -> 20.8 us
  between operations: 14.1 us -> 0.11 us
  matrix products: 10.1 us -> 0 us
    unnamed x1 -> x0, blocking collectives: 255 us -> none
    all_gather x1 -> x0, waiting for transfers between devices: 189 us -> none  [shards(): lax.all_gather(features, 'ex', axis=0, tiled=True)]
    all_gather x0 -> x1, blocking collectives: none -> 55.9 us  [shards(): lax.all_gather(own.astype(jnp.float16), 'z', axis=0, tiled=True)]
    all_to_all x0 -> x1, blocking collectives: none -> 28.5 us  [shards(): lax.all_to_all(parts.astype(jnp.float16), ('xh', 'co', 'yl', 'xl'), 0, 0)]
    ppermute x0 -> x5, starting transfers between devices: none -> 20.8 us  [the longest x1 8.79 us: shards(): across = lax.ppermute(scaled, 'co', [(0, 1), (1, 0)])]
    psum x1 -> x0, blocking collectives: 15 us -> none  [shards(): row_norms = lax.psum(local_squares, 'feat')]
    dot_general x1 -> x0, matrix products: 10.1 us -> none  [inner_tile(): lax.dot_general(left, right, (((1,), (1,)), ((), ())), preferred_element_...]
  transfers between devices with their start and end apart: 2 -> 5, of which waited for: 1 -> 0; matrix products, arithmetic and copies ran while one was open for 0% -> 1% of each run, Pallas kernels for 0% -> 0%
where the time goes in v2:
time: 112 us
  blocking collectives  84.4 us (75%)
  starting transfers between devices  20.8 us (19%)
  Pallas kernels  3.86 us (3%)
  other arithmetic  1.56 us (1%)
    all_gather x1, blocking collectives, shards(): lax.all_gather(own.astype(jnp.float16), 'z', axis=0, tiled=True)  55.9 us
    all_to_all x1, blocking collectives, shards(): lax.all_to_all(parts.astype(jnp.float16), ('xh', 'co', 'yl', 'xl'), 0, 0)  28.5 us
    ppermute x1, starting transfers between devices, shards(): across = lax.ppermute(scaled, 'co', [(0, 1), (1, 0)])  8.79 us
    ppermute x1, starting transfers between devices, shards(): other_across = lax.ppermute(across, ('xh', 'yh'), to_other)  7.51 us
    ppermute x1, starting transfers between devices, shards(): other = lax.ppermute(scaled, ('xh', 'yh'), to_other)  3.2 us
    pallas_call x1, Pallas kernels, shards(): pl.pallas_call(partial_kernel, out_shape=jax.ShapeDtypeStruct((4 * groups...  2.38 us
  transfers between devices with their start and end apart: 5, of which 0 were waited for; matrix products, arithmetic and copies ran while one was open for 1% of the time, Pallas kernels for 0%

profile of v2, /device:TPU:1, one launch (start us, length us, event | category | flops | bytes accessed | tf_op | source)
XLA Modules:
  0.0 111.7 jit_solution(12273904522165452578)
XLA Ops:
  0.0 0.0 copy-start
  0.0 0.9 copy-done
  0.9 0.3 shard_map.17
  1.2 8.8 %collective-permute-start.2 = (bf16[112,1024]{1,0:T(8,128)(2,1)S(1)}, bf16[112,1024]{1,0:T(8,128)(2,1)S(1)}, u32[]{:S(2)}, u32[]{:S(2)}) collective-permute-start(bf16[112,1024]{1,0:T(8,128)(2,1)S(1)} %shard_map.17), channel_id=1, source_target_pairs={{0,8},{8,0},{1,9},{9,1},{2,10},{10,2},{3,11},{11,3},{4,12},{12,4},... | collective-permute-start | bytes 688136 | tf_op jit(solution)/shard_map/ppermute | solution.py:137
  10.0 0.7 collective-permute-start
  10.7 3.2 %collective-permute-start.1 = (bf16[112,1024]{1,0:T(8,128)(2,1)S(1)}, bf16[112,1024]{1,0:T(8,128)(2,1)S(1)}, u32[]{:S(2)}, u32[]{:S(2)}) collective-permute-start(bf16[112,1024]{1,0:T(8,128)(2,1)S(1)} %shard_map.17), channel_id=1, source_target_pairs={{0,4},{4,260},{256,0},{260,256},{1,5},{5,261},{257,1},{261,257},{2... | collective-permute-start | bytes 688136 | tf_op jit(solution)/shard_map/ppermute | solution.py:138
  13.9 0.1 pad_add_fusion.where_ref
  14.0 0.0 collective-permute-done.2
  14.0 0.7 collective-permute-start.3
  14.7 7.5 %collective-permute-start.4 = (bf16[112,1024]{1,0:T(8,128)(2,1)S(1)}, bf16[112,1024]{1,0:T(8,128)(2,1)S(1)}, u32[]{:S(2)}, u32[]{:S(2)}) collective-permute-start(bf16[112,1024]{1,0:T(8,128)(2,1)S(1)} %collective-permute-done.2), channel_id=1, source_target_pairs={{0,4},{4,260},{256,0},{260,256},{1,5},{5,261},{257,1},{261,257},{2... | collective-permute-start | bytes 688136 | tf_op jit(solution)/shard_map/ppermute | solution.py:140
  22.2 0.0 collective-permute-done.refs_0_
  22.2 55.9 %all-gather.1 = f16[1792,1024]{1,0:T(8,128)(2,1)S(1)} all-gather(f16[112,1024]{1,0:T(8,128)(2,1)S(1)} %convert_element_type.12), channel_id=1, replica_groups=mesh['xh'=2,'z'=16,'co'=2,'yh'=2,'yl'=2,'xl'=2] {'z'}, dimensions={0}, use_global_device_ids=true | all-gather | bytes 3899392 | tf_op jit(solution)/shard_map/all_gather | solution.py:141
  78.1 1.1 convert_element_type.13.refs_4_
  79.2 0.0 collective-permute-done.1.refs_1_
  79.2 0.0 collective-permute-done.3.refs_2_
  79.2 0.0 collective-permute-done.4.refs_3_
  79.2 2.4 %shard_map.18 = f32[16,104,384]{2,1,0:T(8,128)S(1)} custom-call(s32[4]{0:T(128)S(1)} %pad_add_fusion.where_ref, bf16[112,1024]{1,0:T(8,128)(2,1)S(1)} %collective-permute-done.refs_0_, bf16[112,1024]{1,0:T(8,128)(2,1)S(1)} %collective-permute-done.1.refs_1_, bf16[112,1024]{1,0:T(8,128)(2,1)S(1)} %collective-permute-done.3.refs_2_, ...), custom_call_target="tpu_custom_call" | custom-call | tf_op jit(solution)/shard_map/pallas_call | solution.py:145
  81.6 0.2 convert_element_type.14
  81.8 28.5 %all_to_all.5 = f16[16,104,384]{2,1,0:T(8,128)(2,1)S(1)} all-to-all(f16[16,104,384]{2,1,0:T(8,128)(2,1)S(1)} %convert_element_type.14), channel_id=1, replica_groups=mesh['xh'=2,'z'=16,'co'=2,'yh'=2,'yl'=2,'xl'=2] {'xh','co','yl','xl'}, dimensions={0} | all-to-all | bytes 2555904 | tf_op jit(solution)/shard_map/all_to_all | solution.py:157
  110.4 0.2 convert_element_type.15.parts_ref
  110.5 1.2 %shard_map.19 = f32[96,768]{1,0:T(8,128)} custom-call(f32[16,104,384]{2,1,0:T(8,128)S(1)} %convert_element_type.15.parts_ref), custom_call_target="tpu_custom_call" | custom-call | tf_op jit(solution)/shard_map/pallas_call | solution.py:158
  (1 shorter events, 0.0 us)
Async XLA Ops:
  0.0 0.9 copy-start
  1.2 12.8 %collective-permute-start.2 = (bf16[112,1024]{1,0:T(8,128)(2,1)S(1)}, bf16[112,1024]{1,0:T(8,128)(2,1)S(1)}, u32[]{:S(2)}, u32[]{:S(2)}) collective-permute-start(bf16[112,1024]{1,0:T(8,128)(2,1)S(1)} %shard_map.17), channel_id=1, source_target_pairs={{0,8},{8,0},{1,9},{9,1},{2,10},{10,2},{3,11},{11,3},{4,12},{12,4},... | collective-permute-start | bytes 688136 | tf_op jit(solution)/shard_map/ppermute | solution.py:137
  10.0 12.2 %collective-permute-start = (bf16[112,1024]{1,0:T(8,128)(2,1)S(1)}, bf16[112,1024]{1,0:T(8,128)(2,1)S(1)}, u32[]{:S(2)}, u32[]{:S(2)}) collective-permute-start(bf16[112,1024]{1,0:T(8,128)(2,1)S(1)} %shard_map.17), channel_id=1, source_target_pairs={{0,0},{4,256},{256,4},{260,260},{1,1},{5,257},{257,5},{261,261},{2... | collective-permute-start | bytes 688136 | tf_op jit(solution)/shard_map/ppermute | solution.py:136
  10.7 68.5 %collective-permute-start.1 = (bf16[112,1024]{1,0:T(8,128)(2,1)S(1)}, bf16[112,1024]{1,0:T(8,128)(2,1)S(1)}, u32[]{:S(2)}, u32[]{:S(2)}) collective-permute-start(bf16[112,1024]{1,0:T(8,128)(2,1)S(1)} %shard_map.17), channel_id=1, source_target_pairs={{0,4},{4,260},{256,0},{260,256},{1,5},{5,261},{257,1},{261,257},{2... | collective-permute-start | bytes 688136 | tf_op jit(solution)/shard_map/ppermute | solution.py:138
  14.0 65.2 %collective-permute-start.3 = (bf16[112,1024]{1,0:T(8,128)(2,1)S(1)}, bf16[112,1024]{1,0:T(8,128)(2,1)S(1)}, u32[]{:S(2)}, u32[]{:S(2)}) collective-permute-start(bf16[112,1024]{1,0:T(8,128)(2,1)S(1)} %collective-permute-done.2), channel_id=1, source_target_pairs={{0,0},{4,256},{256,4},{260,260},{1,1},{5,257},{257,5},{261,261},{2... | collective-permute-start | bytes 688136 | tf_op jit(solution)/shard_map/ppermute | solution.py:139
  14.7 64.5 %collective-permute-start.4 = (bf16[112,1024]{1,0:T(8,128)(2,1)S(1)}, bf16[112,1024]{1,0:T(8,128)(2,1)S(1)}, u32[]{:S(2)}, u32[]{:S(2)}) collective-permute-start(bf16[112,1024]{1,0:T(8,128)(2,1)S(1)} %collective-permute-done.2), channel_id=1, source_target_pairs={{0,4},{4,260},{256,0},{260,256},{1,5},{5,261},{257,1},{261,257},{2... | collective-permute-start | bytes 688136 | tf_op jit(solution)/shard_map/ppermute | solution.py:140

commit v3 on v2

--- a/solution.py
+++ b/solution.py
@@ -1,3 +1,5 @@
+import itertools
+
 import jax
 import jax.numpy as jnp
 from jax import lax
@@ -130,14 +132,14 @@
         out_specs=in_vmem,
         compiler_params=params,
     )(features)
-    pairs = [(a, b) for a in range(2) for b in range(2)]
-    to_own = [(2 * a + b, 2 * b + a) for a, b in pairs]
-    to_other = [(2 * a + b, 2 * b + 1 - a) for a, b in pairs]
-    own = lax.ppermute(scaled, ("xh", "yh"), to_own)
-    across = lax.ppermute(scaled, "co", [(0, 1), (1, 0)])
-    other = lax.ppermute(scaled, ("xh", "yh"), to_other)
-    own_across = lax.ppermute(across, ("xh", "yh"), to_own)
-    other_across = lax.ppermute(across, ("xh", "yh"), to_other)
+    def moved(own, across):
+        pairs = []
+        for a, c, b in itertools.product(range(2), repeat=3):
+            to = ({(0, 0): (1, 0), (0, 1): (0, 0), (1, 1): (0, 1), (1, 0): (1, 1)} if own else {(a, b): (1 - b, 1 - a)})[a, b]
+            pairs.append(((a * 2 + c) * 2 + b, (to[0] * 2 + (c ^ across)) * 2 + to[1]))
+        return lax.ppermute(scaled, ("xh", "co", "yh"), pairs)
+
+    own, own_across, other, other_across = moved(1, 0), moved(1, 1), moved(0, 0), moved(0, 1)
     columns = lax.all_gather(own.astype(jnp.float16), "z", axis=0, tiled=True).astype(jnp.bfloat16)
     yh, co = lax.axis_index("yh"), lax.axis_index("co")
     where = jnp.stack([2 * yh + co, 2 * (1 - yh) + co, 2 * yh + 1 - co, 2 * (1 - yh) + 1 - co]).astype(jnp.int32)

time: 112 us -> 109 us (0.973)
  blocking collectives: 84.4 us -> 82.5 us
    all_to_all x1, blocking collectives: 28.5 us -> 27.4 us  [shards(): lax.all_to_all(parts.astype(jnp.float16), ('xh', 'co', 'yl', 'xl'), 0, 0)]
    ppermute x5 -> x4, starting transfers between devices: 20.8 us -> 20.1 us  [moved(): return lax.ppermute(scaled, ('xh', 'co', 'yh'), pairs)]
  transfers between devices with their start and end apart: 5 -> 4, of which waited for: 0 -> 0; matrix products, arithmetic and copies ran while one was open for 1% -> 1% of each run, Pallas kernels for 0% -> 0%
where the time goes in v3:
time: 109 us
  blocking collectives  82.5 us (76%)
  starting transfers between devices  20.1 us (18%)
  Pallas kernels  3.86 us (4%)
  other arithmetic  1.56 us (1%)
    all_gather x1, blocking collectives, shards(): lax.all_gather(own.astype(jnp.float16), 'z', axis=0, tiled=True)  55.1 us
    all_to_all x1, blocking collectives, shards(): lax.all_to_all(parts.astype(jnp.float16), ('xh', 'co', 'yl', 'xl'), 0, 0)  27.4 us
    ppermute x4, starting transfers between devices, moved(): return lax.ppermute(scaled, ('xh', 'co', 'yh'), pairs)  20.1 us
    pallas_call x1, Pallas kernels, shards(): pl.pallas_call(partial_kernel, out_shape=jax.ShapeDtypeStruct((4 * groups...  2.39 us
  transfers between devices with their start and end apart: 4, of which 0 were waited for; matrix products, arithmetic and copies ran while one was open for 1% of the time, Pallas kernels for 0%

profile of v3, /device:TPU:1, one launch (start us, length us, event | category | flops | bytes accessed | tf_op | source)
XLA Modules:
  0.0 109.0 jit_solution(5091789090051057832)
XLA Ops:
  0.0 0.0 copy-start
  0.0 0.9 copy-done
  0.9 0.3 shard_map.17
  1.2 5.5 %collective-permute-start = (bf16[112,1024]{1,0:T(8,128)(2,1)S(1)}, bf16[112,1024]{1,0:T(8,128)(2,1)S(1)}, u32[]{:S(2)}, u32[]{:S(2)}) collective-permute-start(bf16[112,1024]{1,0:T(8,128)(2,1)S(1)} %shard_map.17), channel_id=1, source_target_pairs={{0,256},{4,0},{8,264},{12,8},{256,260},{260,4},{264,268},{268,12},... | collective-permute-start | bytes 688136 | tf_op jit(solution)/shard_map/ppermute | solution.py:140
  6.7 4.8 %collective-permute-start.1 = (bf16[112,1024]{1,0:T(8,128)(2,1)S(1)}, bf16[112,1024]{1,0:T(8,128)(2,1)S(1)}, u32[]{:S(2)}, u32[]{:S(2)}) collective-permute-start(bf16[112,1024]{1,0:T(8,128)(2,1)S(1)} %shard_map.17), channel_id=1, source_target_pairs={{0,260},{4,4},{8,268},{12,12},{256,256},{260,0},{264,264},{268,8},... | collective-permute-start | bytes 688136 | tf_op jit(solution)/shard_map/ppermute | solution.py:140
  11.5 1.9 %collective-permute-start.2 = (bf16[112,1024]{1,0:T(8,128)(2,1)S(1)}, bf16[112,1024]{1,0:T(8,128)(2,1)S(1)}, u32[]{:S(2)}, u32[]{:S(2)}) collective-permute-start(bf16[112,1024]{1,0:T(8,128)(2,1)S(1)} %shard_map.17), channel_id=1, source_target_pairs={{0,264},{4,8},{8,256},{12,0},{256,268},{260,12},{264,260},{268,4},... | collective-permute-start | bytes 688136 | tf_op jit(solution)/shard_map/ppermute | solution.py:140
  13.4 7.9 %collective-permute-start.3 = (bf16[112,1024]{1,0:T(8,128)(2,1)S(1)}, bf16[112,1024]{1,0:T(8,128)(2,1)S(1)}, u32[]{:S(2)}, u32[]{:S(2)}) collective-permute-start(bf16[112,1024]{1,0:T(8,128)(2,1)S(1)} %shard_map.17), channel_id=1, source_target_pairs={{0,268},{4,12},{8,260},{12,4},{256,264},{260,8},{264,256},{268,0},... | collective-permute-start | bytes 688136 | tf_op jit(solution)/shard_map/ppermute | solution.py:140
  21.3 0.1 pad_add_fusion.where_ref
  21.4 0.0 collective-permute-done.refs_0_
  21.5 55.1 %all-gather.1 = f16[1792,1024]{1,0:T(8,128)(2,1)S(1)} all-gather(f16[112,1024]{1,0:T(8,128)(2,1)S(1)} %convert_element_type.12), channel_id=1, replica_groups=mesh['xh'=2,'z'=16,'co'=2,'yh'=2,'yl'=2,'xl'=2] {'z'}, dimensions={0}, use_global_device_ids=true | all-gather | bytes 3899392 | tf_op jit(solution)/shard_map/all_gather | solution.py:143
  76.6 1.1 convert_element_type.13.refs_4_
  77.7 0.0 collective-permute-done.1.refs_1_
  77.7 0.0 collective-permute-done.2.refs_2_
  77.7 0.0 collective-permute-done.3.refs_3_
  77.7 2.4 %shard_map.18 = f32[16,104,384]{2,1,0:T(8,128)S(1)} custom-call(s32[4]{0:T(128)S(1)} %pad_add_fusion.where_ref, bf16[112,1024]{1,0:T(8,128)(2,1)S(1)} %collective-permute-done.refs_0_, bf16[112,1024]{1,0:T(8,128)(2,1)S(1)} %collective-permute-done.1.refs_1_, bf16[112,1024]{1,0:T(8,128)(2,1)S(1)} %collective-permute-done.2.refs_2_, ...), custom_call_target="tpu_custom_call" | custom-call | tf_op jit(solution)/shard_map/pallas_call | solution.py:147
  80.1 0.2 convert_element_type.14
  80.3 27.4 %all_to_all.5 = f16[16,104,384]{2,1,0:T(8,128)(2,1)S(1)} all-to-all(f16[16,104,384]{2,1,0:T(8,128)(2,1)S(1)} %convert_element_type.14), channel_id=1, replica_groups=mesh['xh'=2,'z'=16,'co'=2,'yh'=2,'yl'=2,'xl'=2] {'xh','co','yl','xl'}, dimensions={0} | all-to-all | bytes 2555904 | tf_op jit(solution)/shard_map/all_to_all | solution.py:159
  107.7 0.2 convert_element_type.15.parts_ref
  107.8 1.2 %shard_map.19 = f32[96,768]{1,0:T(8,128)} custom-call(f32[16,104,384]{2,1,0:T(8,128)S(1)} %convert_element_type.15.parts_ref), custom_call_target="tpu_custom_call" | custom-call | tf_op jit(solution)/shard_map/pallas_call | solution.py:160
  (1 shorter events, 0.0 us)
Async XLA Ops:
  0.0 0.9 copy-start
  1.2 20.2 %collective-permute-start = (bf16[112,1024]{1,0:T(8,128)(2,1)S(1)}, bf16[112,1024]{1,0:T(8,128)(2,1)S(1)}, u32[]{:S(2)}, u32[]{:S(2)}) collective-permute-start(bf16[112,1024]{1,0:T(8,128)(2,1)S(1)} %shard_map.17), channel_id=1, source_target_pairs={{0,256},{4,0},{8,264},{12,8},{256,260},{260,4},{264,268},{268,12},... | collective-permute-start | bytes 688136 | tf_op jit(solution)/shard_map/ppermute | solution.py:140
  6.7 71.0 %collective-permute-start.1 = (bf16[112,1024]{1,0:T(8,128)(2,1)S(1)}, bf16[112,1024]{1,0:T(8,128)(2,1)S(1)}, u32[]{:S(2)}, u32[]{:S(2)}) collective-permute-start(bf16[112,1024]{1,0:T(8,128)(2,1)S(1)} %shard_map.17), channel_id=1, source_target_pairs={{0,260},{4,4},{8,268},{12,12},{256,256},{260,0},{264,264},{268,8},... | collective-permute-start | bytes 688136 | tf_op jit(solution)/shard_map/ppermute | solution.py:140
  11.5 66.2 %collective-permute-start.2 = (bf16[112,1024]{1,0:T(8,128)(2,1)S(1)}, bf16[112,1024]{1,0:T(8,128)(2,1)S(1)}, u32[]{:S(2)}, u32[]{:S(2)}) collective-permute-start(bf16[112,1024]{1,0:T(8,128)(2,1)S(1)} %shard_map.17), channel_id=1, source_target_pairs={{0,264},{4,8},{8,256},{12,0},{256,268},{260,12},{264,260},{268,4},... | collective-permute-start | bytes 688136 | tf_op jit(solution)/shard_map/ppermute | solution.py:140
  13.4 64.3 %collective-permute-start.3 = (bf16[112,1024]{1,0:T(8,128)(2,1)S(1)}, bf16[112,1024]{1,0:T(8,128)(2,1)S(1)}, u32[]{:S(2)}, u32[]{:S(2)}) collective-permute-start(bf16[112,1024]{1,0:T(8,128)(2,1)S(1)} %shard_map.17), channel_id=1, source_target_pairs={{0,268},{4,12},{8,260},{12,4},{256,264},{260,8},{264,256},{268,0},... | collective-permute-start | bytes 688136 | tf_op jit(solution)/shard_map/ppermute | solution.py:140

commit v4 on v0

v4 whole, which is shorter than its diff:
```python
import jax
import jax.numpy as jnp
from jax import lax
from jax.experimental import pallas as pl
from jax.experimental.pallas import tpu as pltpu
from jax.sharding import Mesh, PartitionSpec as P

AXES = ("xh", "z", "co", "yh", "yl", "xl")
SIZES = (2, 16, 2, 2, 2, 2)
ROWS = 96
HALF = 48
INFO = 16
DEPTH = 1024
PLANES = 16
GROUP = 4
GROUPS = PLANES // GROUP
WIDTH = GROUP * HALF
EPS = 1e-06
LANES = 128
TOP = 16384.0
FIRST_EXPONENT = 7
NORM_UNIT = 32.0
LIFT = 16384.0


def wide(left, right):
    return lax.dot_general(left, right, (((1,), (1,)), ((), ())), preferred_element_type=jnp.float32)


def on_diagonal(rows, lanes, shift=0):
    row = lax.broadcasted_iota(jnp.int32, (rows, lanes), 0)
    return row + shift == lax.broadcasted_iota(jnp.int32, (rows, lanes), 1)


def rounded(x):
    return x.astype(jnp.bfloat16).astype(jnp.float32)


def three_parts(along):
    high = rounded(along)
    middle = rounded((along - high) * 256.0)
    low = rounded((along - high - middle * (1.0 / 256.0)) * 65536.0)
    return high, middle, low


def stacked(parts, rows, lanes):
    row = lax.broadcasted_iota(jnp.int32, (rows, lanes), 0)
    out = jnp.zeros((rows, lanes), jnp.float32)
    for i, part in enumerate(parts):
        out = jnp.where(row == i, part, out)
    return out


def exponent_for(largest):
    scale = jnp.full(largest.shape, 2.0**FIRST_EXPONENT, jnp.float32)
    exponent = jnp.full(largest.shape, float(FIRST_EXPONENT), jnp.float32)
    for bit in (32, 16, 8, 4, 2, 1):
        fits = largest * scale * 2.0**bit < TOP
        scale = jnp.where(fits, scale * 2.0**bit, scale)
        exponent = jnp.where(fits, exponent + bit, exponent)
    return scale, exponent


def scale_kernel(yh_ref, x_ref, first_ref, second_ref):
    values = x_ref[...].astype(jnp.float32)
    largest = jnp.max(jnp.max(jnp.abs(values), axis=1, keepdims=True), axis=0, keepdims=True)
    scale, exponent = exponent_for(largest)
    scaled = values * scale
    norms = jnp.sqrt(jnp.sum(scaled * scaled, axis=1, keepdims=True)) * (1.0 / NORM_UNIT)
    infos = []
    for half in range(2):
        at = half * HALF
        along = jnp.sum(
            jnp.where(on_diagonal(HALF, LANES), norms[at : at + HALF], 0.0), axis=0, keepdims=True
        )
        infos.append(stacked((*three_parts(along), exponent), INFO, LANES))
    whole = scaled.astype(jnp.bfloat16)
    flipped = yh_ref[0] == 1

    def fill(ref, half):
        ref[0:HALF] = whole[half * HALF : (half + 1) * HALF]
        ref[HALF : HALF + INFO] = jnp.zeros((INFO, DEPTH), jnp.bfloat16)
        ref[HALF : HALF + INFO, 0:LANES] = infos[half].astype(jnp.bfloat16)

    @pl.when(jnp.logical_not(flipped))
    def _():
        fill(first_ref, 0)
        fill(second_ref, 1)

    @pl.when(flipped)
    def _():
        fill(first_ref, 1)
        fill(second_ref, 0)


def scaled_norm(info):
    return (info[0:1] + info[1:2] * (1.0 / 256.0) + info[2:3] * (1.0 / 65536.0)) * NORM_UNIT


def inverse(norm):
    return jnp.where(norm > 0.0, 1.0 / jnp.where(norm > 0.0, norm, 1.0), 0.0)


def encoded(norm):
    scale, exponent = exponent_for(norm * (1.0 / NORM_UNIT))
    return (*three_parts(norm * scale * (1.0 / NORM_UNIT)), exponent)


def partial_kernel(xh_ref, rows_ref, cols_ref, info_ref, out_ref, left_ref, lanes_ref):
    xh = xh_ref[0]
    squares = []
    for row in range(4):
        both = []
        for i, yh in enumerate((xh, 1 - xh)):
            block = rows_ref[2 * row + yh]
            left_ref[i, row * ROWS : (row + 1) * ROWS] = block
            full = block.astype(jnp.float32)
            both.append(jnp.sum(full * full, axis=1, keepdims=True))
        squares.append(both[0] + both[1])
    for z in range(PLANES):
        lanes_ref[0:8, z * HALF : (z + 1) * HALF] = info_ref[z, 0:8, 0:HALF]
    gram, col_squares = None, None
    for i in range(2):
        block = jnp.concatenate([cols_ref[z, i * HALF : (i + 1) * HALF] for z in range(PLANES)], axis=0)
        info = lanes_ref[4 * i : 4 * i + 4]
        back = jnp.exp2(-info[3:4])
        norm = scaled_norm(info) * back
        product = wide(left_ref[i], block) * back
        gram = product if gram is None else gram + product
        col_squares = norm * norm if col_squares is None else col_squares + norm * norm
    col_norms = jnp.sqrt(col_squares)
    gram = gram * (inverse(col_norms) * LIFT)
    col_info = stacked(encoded(col_norms), 4, PLANES * HALF)
    for row in range(4):
        row_norms = jnp.sqrt(squares[row])
        scaled = gram[row * ROWS : (row + 1) * ROWS] * inverse(row_norms)
        along = jnp.sum(jnp.where(on_diagonal(ROWS, LANES), row_norms, 0.0), axis=0, keepdims=True)
        row_info = stacked(encoded(along), 4, LANES)
        for group in range(GROUPS):
            slot = row * GROUPS + group
            at = group * WIDTH
            for half in range(2):
                lanes = slice(half * WIDTH, (half + 1) * WIDTH)
                out_ref[slot, 0:HALF, lanes] = scaled[half * HALF : (half + 1) * HALF, at : at + WIDTH]
                out_ref[slot, HALF : HALF + 4, lanes] = col_info[:, at : at + WIDTH]
            out_ref[slot, HALF + 4 : HALF + 8, 0:LANES] = row_info


def final_kernel(parts_ref, out_ref):
    left = lax.broadcasted_iota(jnp.int32, (HALF, 2 * WIDTH), 1) < WIDTH

    def weights(slots, first, lanes):
        infos = [parts_ref[slot, first : first + 4, 0:lanes] for slot in slots]
        norms = [scaled_norm(info) * jnp.exp2(-info[3:4]) for info in infos]
        total = norms[0] * norms[0]
        for norm in norms[1:]:
            total += norm * norm
        shrink = lax.rsqrt(total + EPS) * LIFT**-0.5
        return [norm * shrink for norm in norms]

    downs = []
    for along in weights(range(4), HALF + 4, LANES):
        top, bottom = [
            jnp.sum(jnp.where(on_diagonal(HALF, LANES, at), along, 0.0), axis=1, keepdims=True) for at in (0, HALF)
        ]
        downs.append(jnp.where(left, top, bottom))
    for xh in range(2):
        for core in range(2):
            slots = [(xh * 2 + core) * 4 + low for low in range(4)]
            total = None
            for slot, down, across in zip(slots, downs, weights(slots, HALF, 2 * WIDTH)):
                term = parts_ref[slot, 0:HALF] * down * across
                total = term if total is None else total + term
            for low in range(GROUP):
                at = (low * 2 + core) * ROWS + xh * HALF
                for half in range(2):
                    source = half * WIDTH + low * HALF
                    out_ref[half * HALF : (half + 1) * HALF, at : at + HALF] = total[:, source : source + HALF]


def shards(features):
    in_vmem = pl.BlockSpec(memory_space=pltpu.VMEM)
    in_smem = pl.BlockSpec(memory_space=pltpu.SMEM)
    params = pltpu.CompilerParams(vmem_limit_bytes=40 << 20)
    xh, yh = (lax.axis_index(name).astype(jnp.int32).reshape(1) for name in ("xh", "yh"))
    half_block = jax.ShapeDtypeStruct((HALF + INFO, DEPTH), jnp.bfloat16)
    first, second = pl.pallas_call(
        scale_kernel,
        out_shape=(half_block, half_block),
        in_specs=[in_smem, in_vmem],
        out_specs=(in_vmem, in_vmem),
        compiler_params=params,
    )(yh, features)
    pairs = [(a, b) for a in range(2) for b in range(2)]
    first = lax.ppermute(first, ("xh", "yh"), [(2 * a + b, 2 * b + a) for a, b in pairs])
    second = lax.ppermute(second, ("xh", "yh"), [(2 * a + b, 2 * (1 - b) + a) for a, b in pairs])
    rows = lax.all_to_all(jnp.broadcast_to(features, (8, ROWS, DEPTH)), ("xh", "co", "yh"), 0, 0)
    block = jnp.concatenate([first[:HALF], second[:HALF], first[HALF : HALF + 4], second[HALF : HALF + 4]], axis=0)
    columns = lax.all_gather(block.astype(jnp.float16), "z", axis=0, tiled=False)
    info = columns[:, ROWS:, :LANES].astype(jnp.float32)
    parts = pl.pallas_call(
        partial_kernel,
        out_shape=jax.ShapeDtypeStruct((4 * GROUPS, HALF + 8, 2 * WIDTH), jnp.float32),
        in_specs=[in_smem] + [in_vmem] * 3,
        out_specs=in_vmem,
        scratch_shapes=[
            pltpu.VMEM((2, 4 * ROWS, DEPTH), jnp.bfloat16),
            pltpu.VMEM((8, PLANES * HALF), jnp.float32),
        ],
        compiler_params=params,
    )(xh, rows, columns.astype(jnp.bfloat16), info)
    parts = lax.all_to_all(parts.astype(jnp.float16), ("xh", "co", "yl", "xl"), 0, 0)
    return pl.pallas_call(
        final_kernel,
        out_shape=jax.ShapeDtypeStruct((ROWS, 4 * WIDTH), jnp.float32),
        in_specs=[in_vmem],
        out_specs=in_vmem,
        compiler_params=params,
    )(parts.astype(jnp.float32))


def solution(mesh):
    split = Mesh(mesh.devices.reshape(SIZES), AXES)
    placed = P(("xh", "z", "co"), ("yh", "yl", "xl"))
    return jax.shard_map(shards, mesh=split, in_specs=(placed,), out_specs=placed, check_vma=False)
```

time: 491 us -> 103 us (0.21)
  blocking collectives: 270 us -> 75.9 us
  waiting for transfers between devices: 190 us -> 0.01 us
  starting transfers between devices: 0.04 us -> 18.5 us
  between operations: 14.1 us -> 0.1 us
  matrix products: 10.1 us -> 0 us
    unnamed x1 -> x0, blocking collectives: 255 us -> none
    all_gather x1 -> x0, waiting for transfers between devices: 189 us -> none  [shards(): lax.all_gather(features, 'ex', axis=0, tiled=True)]
    all_gather x0 -> x1, blocking collectives: none -> 52.8 us  [shards(): lax.all_gather(block.astype(jnp.float16), 'z', axis=0, tiled=False)]
    all_to_all x0 -> x1, blocking collectives: none -> 23.1 us  [shards(): lax.all_to_all(parts.astype(jnp.float16), ('xh', 'co', 'yl', 'xl'), 0, 0)]
    psum x1 -> x0, blocking collectives: 15 us -> none  [shards(): row_norms = lax.psum(local_squares, 'feat')]
    all_to_all x0 -> x1, starting transfers between devices: none -> 12.3 us  [shards(): lax.all_to_all(jnp.broadcast_to(features, (8, ROWS, DEPTH)), ('xh', 'co',...]
    dot_general x1 -> x0, matrix products: 10.1 us -> none  [inner_tile(): lax.dot_general(left, right, (((1,), (1,)), ((), ())), preferred_element_...]
    ppermute x0 -> x2, starting transfers between devices: none -> 6.15 us  [the longest x1 5.48 us: shards(): lax.ppermute(second, ('xh', 'yh'), [(2 * a + b, 2 * (1 - b) + a) for a, b...]
  transfers between devices with their start and end apart: 2 -> 3, of which waited for: 1 -> 0; matrix products, arithmetic and copies ran while one was open for 0% -> 2% of each run, Pallas kernels for 0% -> 0%
where the time goes in v4:
time: 103 us
  blocking collectives  75.9 us (74%)
  starting transfers between devices  18.5 us (18%)
  Pallas kernels  4.6 us (4%)
  local copies, waits for them, and re-layouts  2.3 us (2%)
  other arithmetic  1.25 us (1%)
    all_gather x1, blocking collectives, shards(): lax.all_gather(block.astype(jnp.float16), 'z', axis=0, tiled=False)  52.8 us
    all_to_all x1, blocking collectives, shards(): lax.all_to_all(parts.astype(jnp.float16), ('xh', 'co', 'yl', 'xl'), 0, 0)  23.1 us
    all_to_all x1, starting transfers between devices, shards(): lax.all_to_all(jnp.broadcast_to(features, (8, ROWS, DEPTH)), ('xh', 'co',...  12.3 us
    ppermute x1, starting transfers between devices, shards(): lax.ppermute(second, ('xh', 'yh'), [(2 * a + b, 2 * (1 - b) + a) for a, b...  5.48 us
    pallas_call x1, Pallas kernels, shards(): pl.pallas_call(partial_kernel, out_shape=jax.ShapeDtypeStruct((4 * GROUPS...  3.17 us
  transfers between devices with their start and end apart: 3, of which 0 were waited for; matrix products, arithmetic and copies ran while one was open for 2% of the time, Pallas kernels for 0%

profile of v4, /device:TPU:1, one launch (start us, length us, event | category | flops | bytes accessed | tf_op | source)
XLA Modules:
  0.0 102.6 jit_solution(8535440333712333452)
XLA Ops:
  0.0 0.0 copy-start
  0.0 0.9 copy-done
  0.9 0.3 shard_map.17
  1.2 5.5 %collective-permute-start.1 = (bf16[64,1024]{1,0:T(8,128)(2,1)S(1)}, bf16[64,1024]{1,0:T(8,128)(2,1)S(1)}, u32[]{:S(2)}, u32[]{:S(2)}) collective-permute-start(bf16[64,1024]{1,0:T(8,128)(2,1)S(1)} %get-tuple-element.8), channel_id=1, source_target_pairs={{0,256},{4,0},{256,260},{260,4},{1,257},{5,1},{257,261},{261,5},{2... | collective-permute-start | bytes 393224 | tf_op jit(solution)/shard_map/ppermute | solution.py:196
  6.7 0.7 collective-permute-start
  7.4 1.3 %broadcast_in_dim.3 = bf16[8,96,1024]{2,1,0:T(8,128)(2,1)} broadcast(bf16[96,1024]{1,0:T(8,128)(2,1)S(1)} %copy-done), dimensions={1,2} | broadcast | bytes 1769472 | tf_op jit(solution)/shard_map/broadcast_in_dim | solution.py:197
  8.7 12.3 %all-to-all-start = ((bf16[8,96,1024]{2,1,0:T(8,128)(2,1)}), bf16[8,96,1024]{2,1,0:T(8,128)(2,1)}, u32[]{:S(2)}, u32[]{:S(2)}) async-start(bf16[8,96,1024]{2,1,0:T(8,128)(2,1)} %broadcast_in_dim.3), calls=%async_computation | async-start | bytes 3145728 | tf_op jit(solution)/shard_map/all_to_all | solution.py:197
  21.1 0.0 collective-permute-done.1
  21.1 0.0 collective-permute-done
  21.2 52.8 %all-gather.1 = f16[16,104,1024]{2,1,0:T(8,128)(2,1)S(1)} all-gather(f16[1,104,1024]{2,1,0:T(8,128)(2,1)S(1)} %maximum_convert_fusion), channel_id=1, replica_groups=mesh['xh'=2,'z'=16,'co'=2,'yh'=2,'yl'=2,'xl'=2] {'z'}, dimensions={0}, use_global_device_ids=true | all-gather | bytes 3620864 | tf_op jit(solution)/shard_map/all_gather | solution.py:199
  74.0 1.0 convert_element_type.23.cols_ref
  75.0 0.0 all-to-all-done.rows_ref
  75.0 3.2 %shard_map.18 = f32[16,56,384]{2,1,0:T(8,128)S(1)} custom-call(s32[1]{0:T(128)} %bitcast.xh_ref, bf16[8,96,1024]{2,1,0:T(8,128)(2,1)} %all-to-all-done.rows_ref, bf16[16,104,1024]{2,1,0:T(8,128)(2,1)S(1)} %convert_element_type.23.cols_ref, f32[16,8,128]{2,1,0:T(8,128)S(1)} %slice_convert_fusion.info_ref), custom_call_target="tpu_custom_call" | custom-call | tf_op jit(solution)/shard_map/pallas_call | solution.py:201
  78.2 0.1 convert_element_type.25
  78.3 23.1 %all_to_all.10 = f16[16,56,384]{2,1,0:T(8,128)(2,1)S(1)} all-to-all(f16[16,56,384]{2,1,0:T(8,128)(2,1)S(1)} %convert_element_type.25), channel_id=1, replica_groups=mesh['xh'=2,'z'=16,'co'=2,'yh'=2,'yl'=2,'xl'=2] {'xh','co','yl','xl'}, dimensions={0} | all-to-all | bytes 1376256 | tf_op jit(solution)/shard_map/all_to_all | solution.py:212
  101.4 0.1 convert_element_type.26.parts_ref
  101.5 1.1 %shard_map.19 = f32[96,768]{1,0:T(8,128)} custom-call(f32[16,56,384]{2,1,0:T(8,128)S(1)} %convert_element_type.26.parts_ref), custom_call_target="tpu_custom_call" | custom-call | tf_op jit(solution)/shard_map/pallas_call | solution.py:213
  (6 shorter events, 0.1 us)
Async XLA Ops:
  0.0 0.9 copy-start
  1.2 19.8 %collective-permute-start.1 = (bf16[64,1024]{1,0:T(8,128)(2,1)S(1)}, bf16[64,1024]{1,0:T(8,128)(2,1)S(1)}, u32[]{:S(2)}, u32[]{:S(2)}) collective-permute-start(bf16[64,1024]{1,0:T(8,128)(2,1)S(1)} %get-tuple-element.8), channel_id=1, source_target_pairs={{0,256},{4,0},{256,260},{260,4},{1,257},{5,1},{257,261},{261,5},{2... | collective-permute-start | bytes 393224 | tf_op jit(solution)/shard_map/ppermute | solution.py:196
  6.7 14.4 %collective-permute-start = (bf16[64,1024]{1,0:T(8,128)(2,1)S(1)}, bf16[64,1024]{1,0:T(8,128)(2,1)S(1)}, u32[]{:S(2)}, u32[]{:S(2)}) collective-permute-start(bf16[64,1024]{1,0:T(8,128)(2,1)S(1)} %get-tuple-element.7), channel_id=1, source_target_pairs={{0,0},{4,256},{256,4},{260,260},{1,1},{5,257},{257,5},{261,261},{2... | collective-permute-start | bytes 393224 | tf_op jit(solution)/shard_map/ppermute | solution.py:195
  8.7 66.2 %all-to-all-start = ((bf16[8,96,1024]{2,1,0:T(8,128)(2,1)}), bf16[8,96,1024]{2,1,0:T(8,128)(2,1)}, u32[]{:S(2)}, u32[]{:S(2)}) async-start(bf16[8,96,1024]{2,1,0:T(8,128)(2,1)} %broadcast_in_dim.3), calls=%async_computation | async-start | bytes 3145728 | tf_op jit(solution)/shard_map/all_to_all | solution.py:197

commit v5 on v4

--- a/solution.py
+++ b/solution.py
@@ -1,3 +1,5 @@
+import itertools
+
 import jax
 import jax.numpy as jnp
 from jax import lax
@@ -191,10 +193,20 @@
         out_specs=(in_vmem, in_vmem),
         compiler_params=params,
     )(yh, features)
-    pairs = [(a, b) for a in range(2) for b in range(2)]
-    first = lax.ppermute(first, ("xh", "yh"), [(2 * a + b, 2 * b + a) for a, b in pairs])
-    second = lax.ppermute(second, ("xh", "yh"), [(2 * a + b, 2 * (1 - b) + a) for a, b in pairs])
-    rows = lax.all_to_all(jnp.broadcast_to(features, (8, ROWS, DEPTH)), ("xh", "co", "yh"), 0, 0)
+    firsts, seconds = [], []
+    for a, b, yl in itertools.product(range(2), repeat=3):
+        to = yl if a == b else 1 - yl
+        firsts.append((4 * a + 2 * b + yl, 4 * b + 2 * a + to))
+        seconds.append((4 * a + 2 * b + yl, 4 * (1 - b) + 2 * a + to))
+    first = lax.ppermute(first, ("xh", "yh", "yl"), firsts)
+    second = lax.ppermute(second, ("xh", "yh", "yl"), seconds)
+    groups = [
+        [8 * a + 4 * c + 2 * b + (b ^ mirror) for a, c, b in itertools.product(range(2), repeat=3)]
+        for mirror in range(2)
+    ]
+    rows = lax.all_to_all(
+        jnp.broadcast_to(features, (8, ROWS, DEPTH)), ("xh", "co", "yh", "yl"), 0, 0, axis_index_groups=groups
+    )
     block = jnp.concatenate([first[:HALF], second[:HALF], first[HALF : HALF + 4], second[HALF : HALF + 4]], axis=0)
     columns = lax.all_gather(block.astype(jnp.float16), "z", axis=0, tiled=False)
     info = columns[:, ROWS:, :LANES].astype(jnp.float32)

time: 103 us -> 102 us (level)
  no operation moved by 1% of the time
where the time goes in v5:
time: 102 us
  blocking collectives  75.7 us (74%)
  starting transfers between devices  18.2 us (18%)
  Pallas kernels  4.6 us (5%)
  local copies, waits for them, and re-layouts  2.3 us (2%)
  other arithmetic  1.25 us (1%)
    all_gather x1, blocking collectives, shards(): lax.all_gather(block.astype(jnp.float16), 'z', axis=0, tiled=False)  52.6 us
    all_to_all x1, blocking collectives, shards(): lax.all_to_all(parts.astype(jnp.float16), ('xh', 'co', 'yl', 'xl'), 0, 0)  23.1 us
    all_to_all x1, starting transfers between devices, shards(): lax.all_to_all(jnp.broadcast_to(features, (8, ROWS, DEPTH)), ('xh', 'co',...  12 us
    ppermute x1, starting transfers between devices, shards(): second = lax.ppermute(second, ('xh', 'yh', 'yl'), seconds)  5.48 us
    pallas_call x1, Pallas kernels, shards(): pl.pallas_call(partial_kernel, out_shape=jax.ShapeDtypeStruct((4 * GROUPS...  3.17 us
  transfers between devices with their start and end apart: 3, of which 0 were waited for; matrix products, arithmetic and copies ran while one was open for 2% of the time, Pallas kernels for 0%

profile of v5, /device:TPU:1, one launch (start us, length us, event | category | flops | bytes accessed | tf_op | source)
XLA Modules:
  0.0 102.1 jit_solution(2328033134218694402)
XLA Ops:
  0.0 0.0 copy-start
  0.0 0.9 copy-done
  0.9 0.3 shard_map.17
  1.2 5.5 %collective-permute-start.1 = (bf16[64,1024]{1,0:T(8,128)(2,1)S(1)}, bf16[64,1024]{1,0:T(8,128)(2,1)S(1)}, u32[]{:S(2)}, u32[]{:S(2)}) collective-permute-start(bf16[64,1024]{1,0:T(8,128)(2,1)S(1)} %get-tuple-element.8), channel_id=1, source_target_pairs={{0,256},{2,258},{4,2},{6,0},{256,262},{258,260},{260,4},{262,6},{1... | collective-permute-start | bytes 393224 | tf_op jit(solution)/shard_map/ppermute | solution.py:202
  6.7 0.7 collective-permute-start
  7.4 1.3 %broadcast_in_dim.3 = bf16[8,96,1024]{2,1,0:T(8,128)(2,1)} broadcast(bf16[96,1024]{1,0:T(8,128)(2,1)S(1)} %copy-done), dimensions={1,2} | broadcast | bytes 1769472 | tf_op jit(solution)/shard_map/broadcast_in_dim | solution.py:208
  8.7 12.0 %all-to-all-start = ((bf16[8,96,1024]{2,1,0:T(8,128)(2,1)}), bf16[8,96,1024]{2,1,0:T(8,128)(2,1)}, u32[]{:S(2)}, u32[]{:S(2)}) async-start(bf16[8,96,1024]{2,1,0:T(8,128)(2,1)} %broadcast_in_dim.3), calls=%async_computation | async-start | bytes 3145728 | tf_op jit(solution)/shard_map/all_to_all | solution.py:207
  20.8 0.0 collective-permute-done.1
  20.8 0.0 collective-permute-done
  20.9 52.6 %all-gather.1 = f16[16,104,1024]{2,1,0:T(8,128)(2,1)S(1)} all-gather(f16[1,104,1024]{2,1,0:T(8,128)(2,1)S(1)} %maximum_convert_fusion), channel_id=1, replica_groups=mesh['xh'=2,'z'=16,'co'=2,'yh'=2,'yl'=2,'xl'=2] {'z'}, dimensions={0}, use_global_device_ids=true | all-gather | bytes 3620864 | tf_op jit(solution)/shard_map/all_gather | solution.py:211
  73.5 1.0 convert_element_type.23.cols_ref
  74.5 0.0 all-to-all-done.rows_ref
  74.5 3.2 %shard_map.18 = f32[16,56,384]{2,1,0:T(8,128)S(1)} custom-call(s32[1]{0:T(128)} %bitcast.xh_ref, bf16[8,96,1024]{2,1,0:T(8,128)(2,1)} %all-to-all-done.rows_ref, bf16[16,104,1024]{2,1,0:T(8,128)(2,1)S(1)} %convert_element_type.23.cols_ref, f32[16,8,128]{2,1,0:T(8,128)S(1)} %slice_convert_fusion.info_ref), custom_call_target="tpu_custom_call" | custom-call | tf_op jit(solution)/shard_map/pallas_call | solution.py:213
  77.7 0.1 convert_element_type.25
  77.8 23.1 %all_to_all.10 = f16[16,56,384]{2,1,0:T(8,128)(2,1)S(1)} all-to-all(f16[16,56,384]{2,1,0:T(8,128)(2,1)S(1)} %convert_element_type.25), channel_id=1, replica_groups=mesh['xh'=2,'z'=16,'co'=2,'yh'=2,'yl'=2,'xl'=2] {'xh','co','yl','xl'}, dimensions={0} | all-to-all | bytes 1376256 | tf_op jit(solution)/shard_map/all_to_all | solution.py:224
  100.9 0.1 convert_element_type.26.parts_ref
  101.0 1.1 %shard_map.19 = f32[96,768]{1,0:T(8,128)} custom-call(f32[16,56,384]{2,1,0:T(8,128)S(1)} %convert_element_type.26.parts_ref), custom_call_target="tpu_custom_call" | custom-call | tf_op jit(solution)/shard_map/pallas_call | solution.py:225
  (6 shorter events, 0.1 us)
Async XLA Ops:
  0.0 0.9 copy-start
  1.2 19.5 %collective-permute-start.1 = (bf16[64,1024]{1,0:T(8,128)(2,1)S(1)}, bf16[64,1024]{1,0:T(8,128)(2,1)S(1)}, u32[]{:S(2)}, u32[]{:S(2)}) collective-permute-start(bf16[64,1024]{1,0:T(8,128)(2,1)S(1)} %get-tuple-element.8), channel_id=1, source_target_pairs={{0,256},{2,258},{4,2},{6,0},{256,262},{258,260},{260,4},{262,6},{1... | collective-permute-start | bytes 393224 | tf_op jit(solution)/shard_map/ppermute | solution.py:202
  6.7 14.1 %collective-permute-start = (bf16[64,1024]{1,0:T(8,128)(2,1)S(1)}, bf16[64,1024]{1,0:T(8,128)(2,1)S(1)}, u32[]{:S(2)}, u32[]{:S(2)}) collective-permute-start(bf16[64,1024]{1,0:T(8,128)(2,1)S(1)} %get-tuple-element.7), channel_id=1, source_target_pairs={{0,0},{2,2},{4,258},{6,256},{256,6},{258,4},{260,260},{262,262},{1... | collective-permute-start | bytes 393224 | tf_op jit(solution)/shard_map/ppermute | solution.py:201
  8.7 65.8 %all-to-all-start = ((bf16[8,96,1024]{2,1,0:T(8,128)(2,1)}), bf16[8,96,1024]{2,1,0:T(8,128)(2,1)}, u32[]{:S(2)}, u32[]{:S(2)}) async-start(bf16[8,96,1024]{2,1,0:T(8,128)(2,1)} %broadcast_in_dim.3), calls=%async_computation | async-start | bytes 3145728 | tf_op jit(solution)/shard_map/all_to_all | solution.py:207

commit v6 on v5

--- a/solution.py
+++ b/solution.py
@@ -19,6 +19,8 @@
 WIDTH = GROUP * HALF
 EPS = 1e-06
 LANES = 128
+TILES = DEPTH // LANES
+TALL = TILES * HALF
 TOP = 16384.0
 FIRST_EXPONENT = 7
 NORM_UNIT = 32.0
@@ -80,9 +82,10 @@
     flipped = yh_ref[0] == 1
 
     def fill(ref, half):
-        ref[0:HALF] = whole[half * HALF : (half + 1) * HALF]
-        ref[HALF : HALF + INFO] = jnp.zeros((INFO, DEPTH), jnp.bfloat16)
-        ref[HALF : HALF + INFO, 0:LANES] = infos[half].astype(jnp.bfloat16)
+        for tile in range(TILES):
+            lanes = slice(tile * LANES, (tile + 1) * LANES)
+            ref[tile * HALF : (tile + 1) * HALF] = whole[half * HALF : (half + 1) * HALF, lanes]
+        ref[TALL : TALL + INFO] = infos[half].astype(jnp.bfloat16)
 
     @pl.when(jnp.logical_not(flipped))
     def _():
@@ -108,7 +111,7 @@
     return (*three_parts(norm * scale * (1.0 / NORM_UNIT)), exponent)
 
 
-def partial_kernel(xh_ref, rows_ref, cols_ref, info_ref, out_ref, left_ref, lanes_ref):
+def partial_kernel(xh_ref, rows_ref, cols_ref, info_ref, out_ref, left_ref, right_ref, lanes_ref):
     xh = xh_ref[0]
     squares = []
     for row in range(4):
@@ -121,13 +124,16 @@
         squares.append(both[0] + both[1])
     for z in range(PLANES):
         lanes_ref[0:8, z * HALF : (z + 1) * HALF] = info_ref[z, 0:8, 0:HALF]
+        for i, tile in itertools.product(range(2), range(TILES)):
+            place = right_ref.at[i, z * HALF : (z + 1) * HALF, tile * LANES : (tile + 1) * LANES]
+            at = i * TALL + tile * HALF
+            place[...] = cols_ref[z, at : at + HALF]
     gram, col_squares = None, None
     for i in range(2):
-        block = jnp.concatenate([cols_ref[z, i * HALF : (i + 1) * HALF] for z in range(PLANES)], axis=0)
         info = lanes_ref[4 * i : 4 * i + 4]
         back = jnp.exp2(-info[3:4])
         norm = scaled_norm(info) * back
-        product = wide(left_ref[i], block) * back
+        product = wide(left_ref[i], right_ref[i]) * back
         gram = product if gram is None else gram + product
         col_squares = norm * norm if col_squares is None else col_squares + norm * norm
     col_norms = jnp.sqrt(col_squares)
@@ -185,7 +191,7 @@
     in_smem = pl.BlockSpec(memory_space=pltpu.SMEM)
     params = pltpu.CompilerParams(vmem_limit_bytes=40 << 20)
     xh, yh = (lax.axis_index(name).astype(jnp.int32).reshape(1) for name in ("xh", "yh"))
-    half_block = jax.ShapeDtypeStruct((HALF + INFO, DEPTH), jnp.bfloat16)
+    half_block = jax.ShapeDtypeStruct((TALL + INFO, LANES), jnp.bfloat16)
     first, second = pl.pallas_call(
         scale_kernel,
         out_shape=(half_block, half_block),
@@ -207,9 +213,9 @@
     rows = lax.all_to_all(
         jnp.broadcast_to(features, (8, ROWS, DEPTH)), ("xh", "co", "yh", "yl"), 0, 0, axis_index_groups=groups
     )
-    block = jnp.concatenate([first[:HALF], second[:HALF], first[HALF : HALF + 4], second[HALF : HALF + 4]], axis=0)
+    block = jnp.concatenate([first[:TALL], second[:TALL], first[TALL : TALL + 4], second[TALL : TALL + 4]], axis=0)
     columns = lax.all_gather(block.astype(jnp.float16), "z", axis=0, tiled=False)
-    info = columns[:, ROWS:, :LANES].astype(jnp.float32)
+    info = columns[:, 2 * TALL :].astype(jnp.float32)
     parts = pl.pallas_call(
         partial_kernel,
         out_shape=jax.ShapeDtypeStruct((4 * GROUPS, HALF + 8, 2 * WIDTH), jnp.float32),
@@ -217,6 +223,7 @@
         out_specs=in_vmem,
         scratch_shapes=[
             pltpu.VMEM((2, 4 * ROWS, DEPTH), jnp.bfloat16),
+            pltpu.VMEM((2, PLANES * HALF, DEPTH), jnp.bfloat16),
             pltpu.VMEM((8, PLANES * HALF), jnp.float32),
         ],
         compiler_params=params,

time: 102 us -> 99.7 us (0.977)
  blocking collectives: 75.7 us -> 73.3 us
    all_gather x1, blocking collectives: 52.6 us -> 50.8 us  [shards(): lax.all_gather(block.astype(jnp.float16), 'z', axis=0, tiled=False)]
where the time goes in v6:
time: 99.7 us; the launch traced here: 99.4 us
  blocking collectives  73.3 us (74%)
  starting transfers between devices  18.2 us (18%)
  Pallas kernels  4.77 us (5%)
  local copies, waits for them, and re-layouts  2.29 us (2%)
    all_gather x1, blocking collectives, shards(): lax.all_gather(block.astype(jnp.float16), 'z', axis=0, tiled=False)  50.8 us
    all_to_all x1, blocking collectives, shards(): lax.all_to_all(parts.astype(jnp.float16), ('xh', 'co', 'yl', 'xl'), 0, 0)  22.4 us
    all_to_all x1, starting transfers between devices, shards(): lax.all_to_all(jnp.broadcast_to(features, (8, ROWS, DEPTH)), ('xh', 'co',...  12 us
    ppermute x1, starting transfers between devices, shards(): second = lax.ppermute(second, ('xh', 'yh', 'yl'), seconds)  5.48 us
    pallas_call x1, Pallas kernels, shards(): pl.pallas_call(partial_kernel, out_shape=jax.ShapeDtypeStruct((4 * GROUPS...  3.34 us
  transfers between devices with their start and end apart: 3, of which 0 were waited for; matrix products, arithmetic and copies ran while one was open for 2% of the time, Pallas kernels for 0%

profile of v6, /device:TPU:1, one launch (start us, length us, event | category | flops | bytes accessed | tf_op | source)
XLA Modules:
  0.0 99.4 jit_solution(13810110952704833700)
XLA Ops:
  0.0 0.0 copy-start
  0.0 0.9 copy-done
  0.9 0.3 shard_map.17
  1.2 5.5 %collective-permute-start.1 = (bf16[400,128]{1,0:T(8,128)(2,1)S(1)}, bf16[400,128]{1,0:T(8,128)(2,1)S(1)}, u32[]{:S(2)}, u32[]{:S(2)}) collective-permute-start(bf16[400,128]{1,0:T(8,128)(2,1)S(1)} %get-tuple-element.8), channel_id=1, source_target_pairs={{0,256},{2,258},{4,2},{6,0},{256,262},{258,260},{260,4},{262,6},{1... | collective-permute-start | bytes 307208 | tf_op jit(solution)/shard_map/ppermute | solution.py:208
  6.7 0.7 collective-permute-start
  7.4 1.3 %broadcast_in_dim.3 = bf16[8,96,1024]{2,1,0:T(8,128)(2,1)} broadcast(bf16[96,1024]{1,0:T(8,128)(2,1)S(1)} %copy-done), dimensions={1,2} | broadcast | bytes 1769472 | tf_op jit(solution)/shard_map/broadcast_in_dim | solution.py:214
  8.7 12.0 %all-to-all-start = ((bf16[8,96,1024]{2,1,0:T(8,128)(2,1)}), bf16[8,96,1024]{2,1,0:T(8,128)(2,1)}, u32[]{:S(2)}, u32[]{:S(2)}) async-start(bf16[8,96,1024]{2,1,0:T(8,128)(2,1)} %broadcast_in_dim.3), calls=%async_computation | async-start | bytes 3145728 | tf_op jit(solution)/shard_map/all_to_all | solution.py:213
  20.8 0.0 collective-permute-done.1
  20.8 0.0 collective-permute-done
  20.9 50.8 %all-gather.1 = f16[16,776,128]{2,1,0:T(8,128)(2,1)S(1)} all-gather(f16[1,776,128]{2,1,0:T(8,128)(2,1)S(1)} %maximum_convert_fusion), channel_id=1, replica_groups=mesh['xh'=2,'z'=16,'co'=2,'yh'=2,'yl'=2,'xl'=2] {'z'}, dimensions={0}, use_global_device_ids=true | all-gather | bytes 3377152 | tf_op jit(solution)/shard_map/all_gather | solution.py:217
  71.7 0.5 convert_element_type.23.cols_ref
  72.3 0.0 all-to-all-done.rows_ref
  72.3 3.3 %shard_map.18 = f32[16,56,384]{2,1,0:T(8,128)S(1)} custom-call(s32[1]{0:T(128)} %bitcast.xh_ref, bf16[8,96,1024]{2,1,0:T(8,128)(2,1)} %all-to-all-done.rows_ref, bf16[16,776,128]{2,1,0:T(8,128)(2,1)S(1)} %convert_element_type.23.cols_ref, f32[16,8,128]{2,1,0:T(8,128)S(1)} %slice_convert_fusion.info_ref), custom_call_target="tpu_custom_call" | custom-call | tf_op jit(solution)/shard_map/pallas_call | solution.py:219
  75.6 0.1 convert_element_type.25
  75.8 22.4 %all_to_all.10 = f16[16,56,384]{2,1,0:T(8,128)(2,1)S(1)} all-to-all(f16[16,56,384]{2,1,0:T(8,128)(2,1)S(1)} %convert_element_type.25), channel_id=1, replica_groups=mesh['xh'=2,'z'=16,'co'=2,'yh'=2,'yl'=2,'xl'=2] {'xh','co','yl','xl'}, dimensions={0} | all-to-all | bytes 1376256 | tf_op jit(solution)/shard_map/all_to_all | solution.py:231
  98.2 0.1 convert_element_type.26.parts_ref
  98.3 1.1 %shard_map.19 = f32[96,768]{1,0:T(8,128)} custom-call(f32[16,56,384]{2,1,0:T(8,128)S(1)} %convert_element_type.26.parts_ref), custom_call_target="tpu_custom_call" | custom-call | tf_op jit(solution)/shard_map/pallas_call | solution.py:232
  (6 shorter events, 0.1 us)
Async XLA Ops:
  0.0 0.9 copy-start
  1.2 19.5 %collective-permute-start.1 = (bf16[400,128]{1,0:T(8,128)(2,1)S(1)}, bf16[400,128]{1,0:T(8,128)(2,1)S(1)}, u32[]{:S(2)}, u32[]{:S(2)}) collective-permute-start(bf16[400,128]{1,0:T(8,128)(2,1)S(1)} %get-tuple-element.8), channel_id=1, source_target_pairs={{0,256},{2,258},{4,2},{6,0},{256,262},{258,260},{260,4},{262,6},{1... | collective-permute-start | bytes 307208 | tf_op jit(solution)/shard_map/ppermute | solution.py:208
  6.7 14.1 %collective-permute-start = (bf16[400,128]{1,0:T(8,128)(2,1)S(1)}, bf16[400,128]{1,0:T(8,128)(2,1)S(1)}, u32[]{:S(2)}, u32[]{:S(2)}) collective-permute-start(bf16[400,128]{1,0:T(8,128)(2,1)S(1)} %get-tuple-element.7), channel_id=1, source_target_pairs={{0,0},{2,2},{4,258},{6,256},{256,6},{258,4},{260,260},{262,262},{1... | collective-permute-start | bytes 307208 | tf_op jit(solution)/shard_map/ppermute | solution.py:207
  8.7 63.5 %all-to-all-start = ((bf16[8,96,1024]{2,1,0:T(8,128)(2,1)}), bf16[8,96,1024]{2,1,0:T(8,128)(2,1)}, u32[]{:S(2)}, u32[]{:S(2)}) async-start(bf16[8,96,1024]{2,1,0:T(8,128)(2,1)} %broadcast_in_dim.3), calls=%async_computation | async-start | bytes 3145728 | tf_op jit(solution)/shard_map/all_to_all | solution.py:213

commit v7 on v6

--- a/solution.py
+++ b/solution.py
@@ -111,25 +111,32 @@
     return (*three_parts(norm * scale * (1.0 / NORM_UNIT)), exponent)
 
 
-def partial_kernel(xh_ref, rows_ref, cols_ref, info_ref, out_ref, left_ref, right_ref, lanes_ref):
+def partial_kernel(xh_ref, rows_ref, cols_ref, info_ref, out_ref, left_ref, right_ref, lanes_ref, sems):
     xh = xh_ref[0]
-    squares = []
-    for row in range(4):
-        both = []
-        for i, yh in enumerate((xh, 1 - xh)):
-            block = rows_ref[2 * row + yh]
-            left_ref[i, row * ROWS : (row + 1) * ROWS] = block
-            full = block.astype(jnp.float32)
-            both.append(jnp.sum(full * full, axis=1, keepdims=True))
-        squares.append(both[0] + both[1])
+    copies = [
+        [
+            pltpu.make_async_copy(
+                rows_ref.at[2 * row + yh], left_ref.at[i, pl.ds(row * ROWS, ROWS)], sems.at[i, row]
+            )
+            for row in range(4)
+        ]
+        for i, yh in enumerate((xh, 1 - xh))
+    ]
+    for copy in copies[0] + copies[1]:
+        copy.start()
     for z in range(PLANES):
         lanes_ref[0:8, z * HALF : (z + 1) * HALF] = info_ref[z, 0:8, 0:HALF]
         for i, tile in itertools.product(range(2), range(TILES)):
             place = right_ref.at[i, z * HALF : (z + 1) * HALF, tile * LANES : (tile + 1) * LANES]
             at = i * TALL + tile * HALF
             place[...] = cols_ref[z, at : at + HALF]
-    gram, col_squares = None, None
+    gram, col_squares, squares = None, None, None
     for i in range(2):
+        for copy in copies[i]:
+            copy.wait()
+        full = left_ref[i].astype(jnp.float32)
+        square = jnp.sum(full * full, axis=1, keepdims=True)
+        squares = square if squares is None else squares + square
         info = lanes_ref[4 * i : 4 * i + 4]
         back = jnp.exp2(-info[3:4])
         norm = scaled_norm(info) * back
@@ -140,7 +147,7 @@
     gram = gram * (inverse(col_norms) * LIFT)
     col_info = stacked(encoded(col_norms), 4, PLANES * HALF)
     for row in range(4):
-        row_norms = jnp.sqrt(squares[row])
+        row_norms = jnp.sqrt(squares[row * ROWS : (row + 1) * ROWS])
         scaled = gram[row * ROWS : (row + 1) * ROWS] * inverse(row_norms)
         along = jnp.sum(jnp.where(on_diagonal(ROWS, LANES), row_norms, 0.0), axis=0, keepdims=True)
         row_info = stacked(encoded(along), 4, LANES)
@@ -219,12 +226,13 @@
     parts = pl.pallas_call(
         partial_kernel,
         out_shape=jax.ShapeDtypeStruct((4 * GROUPS, HALF + 8, 2 * WIDTH), jnp.float32),
-        in_specs=[in_smem] + [in_vmem] * 3,
+        in_specs=[in_smem, pl.BlockSpec(memory_space=pl.ANY), in_vmem, in_vmem],
         out_specs=in_vmem,
         scratch_shapes=[
             pltpu.VMEM((2, 4 * ROWS, DEPTH), jnp.bfloat16),
             pltpu.VMEM((2, PLANES * HALF, DEPTH), jnp.bfloat16),
             pltpu.VMEM((8, PLANES * HALF), jnp.float32),
+            pltpu.SemaphoreType.DMA((2, 4)),
         ],
         compiler_params=params,
     )(xh, rows, columns.astype(jnp.bfloat16), info)

time: 99.7 us -> 99.9 us (level)
  no operation moved by 1% of the time
where the time goes in v7:
time: 99.9 us; the launch traced here: 99.7 us
  blocking collectives  73.3 us (73%)
  starting transfers between devices  18.2 us (18%)
  Pallas kernels  5 us (5%)
  local copies, waits for them, and re-layouts  2.29 us (2%)
    all_gather x1, blocking collectives, shards(): lax.all_gather(block.astype(jnp.float16), 'z', axis=0, tiled=False)  50.8 us
    all_to_all x1, blocking collectives, shards(): lax.all_to_all(parts.astype(jnp.float16), ('xh', 'co', 'yl', 'xl'), 0, 0)  22.4 us
    all_to_all x1, starting transfers between devices, shards(): lax.all_to_all(jnp.broadcast_to(features, (8, ROWS, DEPTH)), ('xh', 'co',...  12 us
    ppermute x1, starting transfers between devices, shards(): second = lax.ppermute(second, ('xh', 'yh', 'yl'), seconds)  5.48 us
    pallas_call x1, Pallas kernels, shards(): pl.pallas_call(partial_kernel, out_shape=jax.ShapeDtypeStruct((4 * GROUPS...  3.57 us
  transfers between devices with their start and end apart: 3, of which 0 were waited for; matrix products, arithmetic and copies ran while one was open for 2% of the time, Pallas kernels for 0%

profile of v7, /device:TPU:1, one launch (start us, length us, event | category | flops | bytes accessed | tf_op | source)
XLA Modules:
  0.0 99.7 jit_solution(9320016449348466755)
XLA Ops:
  0.0 0.0 copy-start
  0.0 0.9 copy-done
  0.9 0.3 shard_map.17
  1.2 5.5 %collective-permute-start.1 = (bf16[400,128]{1,0:T(8,128)(2,1)S(1)}, bf16[400,128]{1,0:T(8,128)(2,1)S(1)}, u32[]{:S(2)}, u32[]{:S(2)}) collective-permute-start(bf16[400,128]{1,0:T(8,128)(2,1)S(1)} %get-tuple-element.8), channel_id=1, source_target_pairs={{0,256},{2,258},{4,2},{6,0},{256,262},{258,260},{260,4},{262,6},{1... | collective-permute-start | bytes 307208 | tf_op jit(solution)/shard_map/ppermute | solution.py:215
  6.7 0.7 collective-permute-start
  7.4 1.3 %broadcast_in_dim.3 = bf16[8,96,1024]{2,1,0:T(8,128)(2,1)} broadcast(bf16[96,1024]{1,0:T(8,128)(2,1)S(1)} %copy-done), dimensions={1,2} | broadcast | bytes 1769472 | tf_op jit(solution)/shard_map/broadcast_in_dim | solution.py:221
  8.7 12.0 %all-to-all-start = ((bf16[8,96,1024]{2,1,0:T(8,128)(2,1)}), bf16[8,96,1024]{2,1,0:T(8,128)(2,1)}, u32[]{:S(2)}, u32[]{:S(2)}) async-start(bf16[8,96,1024]{2,1,0:T(8,128)(2,1)} %broadcast_in_dim.3), calls=%async_computation | async-start | bytes 3145728 | tf_op jit(solution)/shard_map/all_to_all | solution.py:220
  20.8 0.0 collective-permute-done.1
  20.8 0.0 collective-permute-done
  20.9 50.8 %all-gather.1 = f16[16,776,128]{2,1,0:T(8,128)(2,1)S(1)} all-gather(f16[1,776,128]{2,1,0:T(8,128)(2,1)S(1)} %maximum_convert_fusion), channel_id=1, replica_groups=mesh['xh'=2,'z'=16,'co'=2,'yh'=2,'yl'=2,'xl'=2] {'z'}, dimensions={0}, use_global_device_ids=true | all-gather | bytes 3377152 | tf_op jit(solution)/shard_map/all_gather | solution.py:224
  71.7 0.5 convert_element_type.23.cols_ref
  72.3 0.0 all-to-all-done.rows_ref
  72.3 3.6 %shard_map.18 = f32[16,56,384]{2,1,0:T(8,128)S(1)} custom-call(s32[1]{0:T(128)} %bitcast.xh_ref, bf16[8,96,1024]{2,1,0:T(8,128)(2,1)} %all-to-all-done.rows_ref, bf16[16,776,128]{2,1,0:T(8,128)(2,1)S(1)} %convert_element_type.23.cols_ref, f32[16,8,128]{2,1,0:T(8,128)S(1)} %slice_convert_fusion.info_ref), custom_call_target="tpu_custom_call" | custom-call | tf_op jit(solution)/shard_map/pallas_call | solution.py:226
  75.9 0.1 convert_element_type.25
  76.0 22.4 %all_to_all.10 = f16[16,56,384]{2,1,0:T(8,128)(2,1)S(1)} all-to-all(f16[16,56,384]{2,1,0:T(8,128)(2,1)S(1)} %convert_element_type.25), channel_id=1, replica_groups=mesh['xh'=2,'z'=16,'co'=2,'yh'=2,'yl'=2,'xl'=2] {'xh','co','yl','xl'}, dimensions={0} | all-to-all | bytes 1376256 | tf_op jit(solution)/shard_map/all_to_all | solution.py:239
  98.4 0.1 convert_element_type.26.parts_ref
  98.5 1.1 %shard_map.19 = f32[96,768]{1,0:T(8,128)} custom-call(f32[16,56,384]{2,1,0:T(8,128)S(1)} %convert_element_type.26.parts_ref), custom_call_target="tpu_custom_call" | custom-call | tf_op jit(solution)/shard_map/pallas_call | solution.py:240
  (6 shorter events, 0.1 us)
Async XLA Ops:
  0.0 0.9 copy-start
  1.2 19.5 %collective-permute-start.1 = (bf16[400,128]{1,0:T(8,128)(2,1)S(1)}, bf16[400,128]{1,0:T(8,128)(2,1)S(1)}, u32[]{:S(2)}, u32[]{:S(2)}) collective-permute-start(bf16[400,128]{1,0:T(8,128)(2,1)S(1)} %get-tuple-element.8), channel_id=1, source_target_pairs={{0,256},{2,258},{4,2},{6,0},{256,262},{258,260},{260,4},{262,6},{1... | collective-permute-start | bytes 307208 | tf_op jit(solution)/shard_map/ppermute | solution.py:215
  6.7 14.1 %collective-permute-start = (bf16[400,128]{1,0:T(8,128)(2,1)S(1)}, bf16[400,128]{1,0:T(8,128)(2,1)S(1)}, u32[]{:S(2)}, u32[]{:S(2)}) collective-permute-start(bf16[400,128]{1,0:T(8,128)(2,1)S(1)} %get-tuple-element.7), channel_id=1, source_target_pairs={{0,0},{2,2},{4,258},{6,256},{256,6},{258,4},{260,260},{262,262},{1... | collective-permute-start | bytes 307208 | tf_op jit(solution)/shard_map/ppermute | solution.py:214
  8.7 63.5 %all-to-all-start = ((bf16[8,96,1024]{2,1,0:T(8,128)(2,1)}), bf16[8,96,1024]{2,1,0:T(8,128)(2,1)}, u32[]{:S(2)}, u32[]{:S(2)}) async-start(bf16[8,96,1024]{2,1,0:T(8,128)(2,1)} %broadcast_in_dim.3), calls=%async_computation | async-start | bytes 3145728 | tf_op jit(solution)/shard_map/all_to_all | solution.py:220

commit v8 on v6

--- a/solution.py
+++ b/solution.py
@@ -96,6 +96,14 @@
     def _():
         fill(first_ref, 1)
         fill(second_ref, 0)
+
+
+def copies_kernel(x_ref, out_ref, sems):
+    copies = [pltpu.make_async_copy(x_ref, out_ref.at[i], sems.at[i]) for i in range(8)]
+    for copy in copies:
+        copy.start()
+    for copy in copies:
+        copy.wait()
 
 
 def scaled_norm(info):
@@ -210,8 +218,16 @@
         [8 * a + 4 * c + 2 * b + (b ^ mirror) for a, c, b in itertools.product(range(2), repeat=3)]
         for mirror in range(2)
     ]
+    copies = pl.pallas_call(
+        copies_kernel,
+        out_shape=jax.ShapeDtypeStruct((8, ROWS, DEPTH), jnp.bfloat16),
+        in_specs=[in_vmem],
+        out_specs=pl.BlockSpec(memory_space=pl.ANY),
+        scratch_shapes=[pltpu.SemaphoreType.DMA((8,))],
+        compiler_params=params,
+    )(features)
     rows = lax.all_to_all(
-        jnp.broadcast_to(features, (8, ROWS, DEPTH)), ("xh", "co", "yh", "yl"), 0, 0, axis_index_groups=groups
+        copies, ("xh", "co", "yh", "yl"), 0, 0, axis_index_groups=groups
     )
     block = jnp.concatenate([first[:TALL], second[:TALL], first[TALL : TALL + 4], second[TALL : TALL + 4]], axis=0)
     columns = lax.all_gather(block.astype(jnp.float16), "z", axis=0, tiled=False)

time: 99.7 us -> 99.6 us (level)
  local copies, waits for them, and re-layouts: 2.29 us -> 0.95 us
  Pallas kernels: 4.77 us -> 6 us
    broadcast_in_dim x1 -> x0, local copies, waits for them, and re-layouts: 1.35 us -> none  [shards(): jnp.broadcast_to(features, (8, ROWS, DEPTH))]
    pallas_call x0 -> x1, Pallas kernels: none -> 1.22 us  [shards(): pl.pallas_call(copies_kernel, out_shape=jax.ShapeDtypeStruct((8, ROWS, DE...]
  transfers between devices with their start and end apart: 3 -> 3, of which waited for: 0 -> 0; matrix products, arithmetic and copies ran while one was open for 2% -> 1% of each run, Pallas kernels for 0% -> 1%
where the time goes in v8:
time: 99.6 us; the launch traced here: 99.3 us
  blocking collectives  73.3 us (74%)
  starting transfers between devices  18.2 us (18%)
  Pallas kernels  6 us (6%)
    all_gather x1, blocking collectives, shards(): lax.all_gather(block.astype(jnp.float16), 'z', axis=0, tiled=False)  50.8 us
    all_to_all x1, blocking collectives, shards(): lax.all_to_all(parts.astype(jnp.float16), ('xh', 'co', 'yl', 'xl'), 0, 0)  22.4 us
    all_to_all x1, starting transfers between devices, shards(): lax.all_to_all(copies, ('xh', 'co', 'yh', 'yl'), 0, 0, axis_index_groups=...  12 us
    ppermute x1, starting transfers between devices, shards(): second = lax.ppermute(second, ('xh', 'yh', 'yl'), seconds)  5.48 us
    pallas_call x1, Pallas kernels, shards(): pl.pallas_call(partial_kernel, out_shape=jax.ShapeDtypeStruct((4 * GROUPS...  3.35 us
  transfers between devices with their start and end apart: 3, of which 0 were waited for; matrix products, arithmetic and copies ran while one was open for 1% of the time, Pallas kernels for 1%

profile of v8, /device:TPU:1, one launch (start us, length us, event | category | flops | bytes accessed | tf_op | source)
XLA Modules:
  0.0 99.3 jit_solution(1502950139235239067)
XLA Ops:
  0.0 0.0 copy-start
  0.0 0.9 copy-done
  0.9 0.3 shard_map.18
  1.2 5.5 %collective-permute-start.1 = (bf16[400,128]{1,0:T(8,128)(2,1)S(1)}, bf16[400,128]{1,0:T(8,128)(2,1)S(1)}, u32[]{:S(2)}, u32[]{:S(2)}) collective-permute-start(bf16[400,128]{1,0:T(8,128)(2,1)S(1)} %get-tuple-element.8), channel_id=1, source_target_pairs={{0,256},{2,258},{4,2},{6,0},{256,262},{258,260},{260,4},{262,6},{1... | collective-permute-start | bytes 307208 | tf_op jit(solution)/shard_map/ppermute | solution.py:216
  6.7 0.7 collective-permute-start
  7.4 1.2 %shard_map.17 = bf16[8,96,1024]{2,1,0:T(8,128)(2,1)} custom-call(bf16[96,1024]{1,0:T(8,128)(2,1)S(1)} %copy-done), custom_call_target="tpu_custom_call" | custom-call | tf_op jit(solution)/shard_map/pallas_call | solution.py:221
  8.6 12.0 %all-to-all-start = ((bf16[8,96,1024]{2,1,0:T(8,128)(2,1)}), bf16[8,96,1024]{2,1,0:T(8,128)(2,1)}, u32[]{:S(2)}, u32[]{:S(2)}) async-start(bf16[8,96,1024]{2,1,0:T(8,128)(2,1)} %shard_map.17), calls=%async_computation | async-start | bytes 3145728 | tf_op jit(solution)/shard_map/all_to_all | solution.py:229
  20.7 0.0 collective-permute-done.1
  20.7 0.0 collective-permute-done
  20.8 50.8 %all-gather.1 = f16[16,776,128]{2,1,0:T(8,128)(2,1)S(1)} all-gather(f16[1,776,128]{2,1,0:T(8,128)(2,1)S(1)} %maximum_convert_fusion), channel_id=1, replica_groups=mesh['xh'=2,'z'=16,'co'=2,'yh'=2,'yl'=2,'xl'=2] {'z'}, dimensions={0}, use_global_device_ids=true | all-gather | bytes 3377152 | tf_op jit(solution)/shard_map/all_gather | solution.py:233
  71.6 0.5 convert_element_type.23.cols_ref
  72.2 0.0 all-to-all-done.rows_ref
  72.2 3.3 %shard_map.19 = f32[16,56,384]{2,1,0:T(8,128)S(1)} custom-call(s32[1]{0:T(128)} %bitcast.xh_ref, bf16[8,96,1024]{2,1,0:T(8,128)(2,1)} %all-to-all-done.rows_ref, bf16[16,776,128]{2,1,0:T(8,128)(2,1)S(1)} %convert_element_type.23.cols_ref, f32[16,8,128]{2,1,0:T(8,128)S(1)} %slice_convert_fusion.info_ref), custom_call_target="tpu_custom_call" | custom-call | tf_op jit(solution)/shard_map/pallas_call | solution.py:235
  75.5 0.1 convert_element_type.25
  75.6 22.4 %all_to_all.10 = f16[16,56,384]{2,1,0:T(8,128)(2,1)S(1)} all-to-all(f16[16,56,384]{2,1,0:T(8,128)(2,1)S(1)} %convert_element_type.25), channel_id=1, replica_groups=mesh['xh'=2,'z'=16,'co'=2,'yh'=2,'yl'=2,'xl'=2] {'xh','co','yl','xl'}, dimensions={0} | all-to-all | bytes 1376256 | tf_op jit(solution)/shard_map/all_to_all | solution.py:247
  98.1 0.1 convert_element_type.26.parts_ref
  98.2 1.1 %shard_map.20 = f32[96,768]{1,0:T(8,128)} custom-call(f32[16,56,384]{2,1,0:T(8,128)S(1)} %convert_element_type.26.parts_ref), custom_call_target="tpu_custom_call" | custom-call | tf_op jit(solution)/shard_map/pallas_call | solution.py:248
  (6 shorter events, 0.1 us)
Async XLA Ops:
  0.0 0.9 copy-start
  1.2 19.4 %collective-permute-start.1 = (bf16[400,128]{1,0:T(8,128)(2,1)S(1)}, bf16[400,128]{1,0:T(8,128)(2,1)S(1)}, u32[]{:S(2)}, u32[]{:S(2)}) collective-permute-start(bf16[400,128]{1,0:T(8,128)(2,1)S(1)} %get-tuple-element.8), channel_id=1, source_target_pairs={{0,256},{2,258},{4,2},{6,0},{256,262},{258,260},{260,4},{262,6},{1... | collective-permute-start | bytes 307208 | tf_op jit(solution)/shard_map/ppermute | solution.py:216
  6.7 14.0 %collective-permute-start = (bf16[400,128]{1,0:T(8,128)(2,1)S(1)}, bf16[400,128]{1,0:T(8,128)(2,1)S(1)}, u32[]{:S(2)}, u32[]{:S(2)}) collective-permute-start(bf16[400,128]{1,0:T(8,128)(2,1)S(1)} %get-tuple-element.7), channel_id=1, source_target_pairs={{0,0},{2,2},{4,258},{6,256},{256,6},{258,4},{260,260},{262,262},{1... | collective-permute-start | bytes 307208 | tf_op jit(solution)/shard_map/ppermute | solution.py:215
  8.6 63.6 %all-to-all-start = ((bf16[8,96,1024]{2,1,0:T(8,128)(2,1)}), bf16[8,96,1024]{2,1,0:T(8,128)(2,1)}, u32[]{:S(2)}, u32[]{:S(2)}) async-start(bf16[8,96,1024]{2,1,0:T(8,128)(2,1)} %shard_map.17), calls=%async_computation | async-start | bytes 3145728 | tf_op jit(solution)/shard_map/all_to_all | solution.py:229
